TPU v7x, 512 devices: a whole 4x4x16 slice. The times are simulated.
512 devices in a mesh: event: 4 (over x), tile: 128 (over z, y, core).
Axes of the slice: x: 4, y: 4, z: 16, core: 2. Of those that a mesh axis runs over, the one named last changes fastest.
Arguments:
- fine: bfloat16 [4, 10240, 32, 256], P('event', 'tile'), may hold values from -6 to 6
- cotangent: bfloat16 [4, 10240, 32, 256], P('event', 'tile'), may hold values from -6 to 6
- counts: int32 [4, 128], P('event', 'tile'), may hold values from 40 to 80, as said below
- parent: int32 [4, 10240], P('event', 'tile'), may hold values from 0 to 2559, as said below
- quadrant: int32 [4, 10240], P('event', 'tile'), may hold values from 0 to 3
- down_weight: bfloat16 [4, 32, 128], replicated, may hold values from -0.5 to 0.5
- mid_weight: bfloat16 [9, 128, 128], replicated, may hold values from -0.1875 to 0.1875
- up_weight: bfloat16 [4, 32, 128], replicated, may hold values from -0.5 to 0.5
Outputs:
- grad_fine: bfloat16 [4, 10240, 32, 256], P('event', 'tile')
- grad_down: float32 [4, 32, 128], replicated
- grad_mid: float32 [9, 128, 128], replicated
- grad_up: float32 [4, 32, 128], replicated
Inputs may be any that keep to these rules, and one draw needn't show every extreme that they name: `counts`: one device of each readout has 80. Among the active tiles of a readout no two share both parent and quadrant. Coarse tile p is owned by device p // 20 along tile. At most 1 active tiles of one device have parents owned by one device, and in every readout some device reaches 1 for some owner.
All inputs are finite; a program needn't handle non-finite values.
Results may differ from a plain program's by a relative error of at most 0.0068.
Values may be sent and summed in bfloat16 or wider, within the bound.
A program may use at most 128 MiB of HBM per device.

v0:
```python
import math

import jax
import jax.numpy as jnp
from jax import lax
from jax.sharding import PartitionSpec as P


def silu_slope(inputs):
    logistic = jax.nn.sigmoid(inputs)
    return logistic * (1.0 + inputs * (1.0 - logistic))


def split_taps(tile_rows):
    number, channels = (tile_rows.shape[0], tile_rows.shape[1])
    blocks = tile_rows.reshape(number, channels, 8, 2, 8, 2)
    return blocks.transpose(0, 2, 4, 3, 5, 1).reshape(number, 64, 4 * channels)


def join_taps(tap_rows, channels):
    number = tap_rows.shape[0]
    blocks = tap_rows.reshape(number, 8, 8, 2, 2, channels)
    return blocks.transpose(0, 5, 1, 3, 2, 4).reshape(number, channels, 256)


def quads_to_grid(quarters):
    number = quarters.shape[0] // 4
    channels = quarters.shape[2]
    blocks = quarters.reshape(number, 2, 2, 8, 8, channels)
    return blocks.transpose(0, 1, 3, 2, 4, 5).reshape(number, 256, channels)


def grid_to_quads(coarse_grid):
    number, channels = (coarse_grid.shape[0], coarse_grid.shape[2])
    blocks = coarse_grid.reshape(number, 2, 8, 2, 8, channels)
    return blocks.transpose(0, 1, 3, 2, 4, 5).reshape(number * 4, 64, channels)


def shifted(coarse_grid, row_off, col_off):
    number, channels = (coarse_grid.shape[0], coarse_grid.shape[2])
    padded = jnp.pad(
        coarse_grid.reshape(number, 16, 16, channels), ((0, 0), (1, 1), (1, 1), (0, 0))
    )
    return padded[:, row_off : row_off + 16, col_off : col_off + 16, :].reshape(
        number, 256, channels
    )


def patches(coarse_grid, flip):
    pieces = []
    for row_off in range(3):
        for col_off in range(3):
            if flip:
                pieces.append(shifted(coarse_grid, 2 - row_off, 2 - col_off))
            else:
                pieces.append(shifted(coarse_grid, row_off, col_off))
    return jnp.concatenate(pieces, axis=2).reshape(-1, 9 * coarse_grid.shape[2])


def shards(fine, cotangent, counts, parent, quadrant, down_weight, mid_weight, up_weight):
    tile_rows = fine[0]
    cot_rows = cotangent[0]
    row_count, fine_ch = (tile_rows.shape[0], tile_rows.shape[1])
    coarse_ch = down_weight.shape[2]
    tile_count = lax.axis_size("tile")
    capacity = -(-row_count // tile_count)
    coarse_dev = row_count // 4
    slot_count = tile_count * capacity
    grad_scale = 1.0 / math.sqrt(lax.axis_size("event") * tile_count * row_count * 64)
    down_flat = down_weight.reshape(4 * fine_ch, coarse_ch)
    up_flat = up_weight.reshape(4 * fine_ch, coarse_ch)
    mid_flat = mid_weight.reshape(9 * coarse_ch, coarse_ch)
    mid_back = jnp.transpose(mid_weight, (0, 2, 1)).reshape(9 * coarse_ch, coarse_ch)
    positions = jnp.arange(row_count, dtype=jnp.int32)
    active = positions < counts[0, 0]
    destination = parent[0] // coarse_dev
    child_cell = parent[0] % coarse_dev * 4 + quadrant[0]
    earlier = (
        (destination[:, None] == destination[None, :])
        & active[None, :]
        & (positions[None, :] < positions[:, None])
    )
    rank_within = jnp.sum(earlier.astype(jnp.int32), axis=1)
    placement = jnp.where(active, destination * capacity + rank_within, slot_count)
    slot_ids = jnp.arange(slot_count, dtype=jnp.int32)
    matches = placement[None, :] == slot_ids[:, None]
    filled = jnp.any(matches, axis=1)
    source = jnp.sum(jnp.where(matches, positions[None, :], 0), axis=1)
    cell_tags = jnp.where(filled, jnp.take(child_cell, source), -1)
    cot_send = jnp.take(cot_rows, source, axis=0)
    pick_back = jnp.minimum(placement, slot_count - 1)
    lead_send = jnp.take(tile_rows, source, axis=0)
    lead_got, cot_got, tag_got = (
        lax.all_to_all(lead_send, "tile", split_axis=0, concat_axis=0, tiled=True),
        lax.all_to_all(cot_send, "tile", split_axis=0, concat_axis=0, tiled=True),
        lax.all_to_all(cell_tags, "tile", split_axis=0, concat_axis=0, tiled=True),
    )
    cell_ids = jnp.arange(4 * coarse_dev, dtype=jnp.int32)
    arrived = tag_got[None, :] == cell_ids[:, None]
    present = jnp.any(arrived, axis=1)
    anchor = jnp.sum(jnp.where(arrived, slot_ids[None, :], 0), axis=1)
    present_mask = present[:, None, None]
    return_pick = jnp.maximum(tag_got, 0)
    lead_quads = jnp.where(
        present_mask, jnp.take(lead_got, anchor, axis=0), jnp.zeros((), lead_got.dtype)
    )
    child_taps = split_taps(lead_quads).reshape(-1, 4 * fine_ch)
    child_pre = jnp.dot(child_taps, down_flat, preferred_element_type=jnp.float32)
    act_quads = jax.nn.silu(child_pre).astype(jnp.bfloat16).reshape(-1, 64, coarse_ch)
    act_grid = quads_to_grid(act_quads)
    act_patch = patches(act_grid, False)
    mid_pre = jnp.dot(act_patch, mid_flat, preferred_element_type=jnp.float32)
    out_grid = (act_grid.reshape(-1, coarse_ch) + jax.nn.silu(mid_pre)).astype(jnp.bfloat16)
    out_quads = grid_to_quads(out_grid.reshape(-1, 256, coarse_ch)).reshape(-1, coarse_ch)
    cot_quads = jnp.where(
        present_mask, jnp.take(cot_got, anchor, axis=0), jnp.zeros((), cot_got.dtype)
    )
    g_taps = split_taps(cot_quads).reshape(-1, 4 * fine_ch)
    grad_out_q = jnp.dot(g_taps, up_flat, preferred_element_type=jnp.float32).astype(jnp.bfloat16)
    grad_up = jnp.dot(g_taps.T, out_quads, preferred_element_type=jnp.float32)
    grad_out_grid = quads_to_grid(grad_out_q.reshape(-1, 64, coarse_ch)).reshape(-1, coarse_ch)
    grad_mid_pre = (grad_out_grid * silu_slope(mid_pre)).astype(jnp.bfloat16)
    grad_mid = jnp.dot(act_patch.T, grad_mid_pre, preferred_element_type=jnp.float32)
    back_patch = patches(grad_mid_pre.reshape(-1, 256, coarse_ch), True)
    grad_act = (
        grad_out_grid + jnp.dot(back_patch, mid_back, preferred_element_type=jnp.float32)
    ).astype(jnp.bfloat16)
    grad_act_q = grid_to_quads(grad_act.reshape(-1, 256, coarse_ch))
    grad_pre = (grad_act_q.reshape(-1, coarse_ch) * silu_slope(child_pre)).astype(jnp.bfloat16)
    grad_down = jnp.dot(child_taps.T, grad_pre, preferred_element_type=jnp.float32)
    fine_back = jnp.dot(grad_pre, down_flat.T, preferred_element_type=jnp.float32)
    grad_child = (cot_quads + join_taps(fine_back.reshape(-1, 64, 4 * fine_ch), fine_ch)).astype(
        jnp.bfloat16
    )
    to_return = jnp.take(grad_child, return_pick, axis=0)
    returned = lax.all_to_all(to_return, "tile", split_axis=0, concat_axis=0, tiled=True)
    grad_tiles = jnp.take(returned, pick_back, axis=0)
    grad_fine = jnp.where(active[:, None, None], grad_tiles, jnp.zeros((), jnp.bfloat16))[None]
    summed = lax.psum(
        (grad_down * grad_scale, grad_mid * grad_scale, grad_up * grad_scale), ("event", "tile")
    )
    return (
        grad_fine,
        summed[0].reshape(4, fine_ch, coarse_ch),
        summed[1].reshape(9, coarse_ch, coarse_ch),
        summed[2].reshape(4, fine_ch, coarse_ch),
    )


def solution(mesh):
    placed = (
        P("event", "tile", None, None),
        P("event", "tile", None, None),
        P("event", "tile"),
        P("event", "tile"),
        P("event", "tile"),
        P(),
        P(),
        P(),
    )
    return jax.shard_map(
        shards,
        mesh=mesh,
        in_specs=placed,
        out_specs=(P("event", "tile", None, None), P(), P(), P()),
        check_vma=False,
    )
```

profile of v0, /device:TPU:1, one launch (start us, length us, event | category | flops | bytes accessed | tf_op | source)
XLA Modules:
  0.0 900.4 jit_solution(17246890941941003557)
XLA Ops:
  9.7 1.2 gather_fusion
  11.0 0.7 copy.59
  11.7 20.6 %all-to-all-start = ((s32[128,1,1]{2,1,0:T(1,128)}), s32[128,1,1]{2,1,0:T(1,128)S(1)}, u32[]{:S(2)}, u32[]{:S(2)}) async-start(s32[128,1,1]{2,1,0:T(1,128)} %copy.59), calls=%async_computation | async-start | bytes 131072 | tf_op jit(solution)/shard_map/all_to_all | solution.py:96
  32.3 2.0 gather_fusion.3
  34.3 2.0 gather_fusion.1
  36.3 4.0 broadcast_select_fusion.1
  40.3 6.8 all-to-all-done
  47.1 106.1 %all_to_all.21 = bf16[128,32,256]{2,1,0:T(8,128)(2,1)} all-to-all(bf16[128,32,256]{2,1,0:T(8,128)(2,1)S(1)} %get-tuple-element.37), channel_id=1, replica_groups=mesh['event'=4,'tile'=128] {'tile'}, dimensions={0} | all-to-all | bytes 4194304 | tf_op jit(solution)/shard_map/all_to_all | solution.py:94
  153.2 10.8 %all-to-all-start.1 = ((bf16[128,32,256]{2,1,0:T(8,128)(2,1)}), bf16[128,32,256]{2,1,0:T(8,128)(2,1)S(1)}, u32[]{:S(2)}, u32[]{:S(2)}) async-start(bf16[128,32,256]{2,1,0:T(8,128)(2,1)} %get-tuple-element.38), calls=%async_computation.1 | async-start | bytes 4194304 | tf_op jit(solution)/shard_map/all_to_all | solution.py:95
  164.0 0.9 copy.66
  164.9 2.3 reduce
  167.6 3.4 gather_fusion.4
  171.0 89.8 %all-to-all-done.1 = bf16[128,32,256]{2,1,0:T(8,128)(2,1)S(1)} async-done(((bf16[128,32,256]{2,1,0:T(8,128)(2,1)}), bf16[128,32,256]{2,1,0:T(8,128)(2,1)S(1)}, u32[]{:S(2)}, u32[]{:S(2)}) %all-to-all-start.1) | async-done | bytes 2097184 | tf_op jit(solution)/shard_map/all_to_all | solution.py:95
  260.8 1.8 gather_fusion.2
  262.6 2.1 select_select_fusion.1
  264.7 3.5 copy.63
  268.2 2.5 copy.60
  270.7 8.8 copy.61
  279.6 9.7 %reshape_reshape.14 = bf16[5120,128]{1,0:T(8,128)(2,1)S(1)} reshape(bf16[80,8,8,2,2,32]{5,4,3,2,1,0:T(2,128)(2,1)} %copy.61) | data formatting | bytes 2621440 | tf_op jit(solution)/shard_map/reshape;reshape | solution.py:118
  290.1 1.8 copy.62
  291.9 11.9 %copy.64 = bf16[80,8,8,2,2,32]{5,4,3,2,1,0:T(2,128)(2,1)} copy(bf16[80,8,8,2,2,32]{0,5,4,2,3,1:T(8,128)(2,1)} %bitcast.130) | data formatting | bytes 2621440 | tf_op jit(solution)/shard_map/transpose | solution.py:17
  303.8 10.4 %reshape_reshape.15 = bf16[5120,128]{1,0:T(8,128)(2,1)} reshape(bf16[80,8,8,2,2,32]{5,4,3,2,1,0:T(2,128)(2,1)} %copy.64) | data formatting | bytes 2621440 | tf_op jit(solution)/shard_map/reshape;reshape | solution.py:107
  314.2 2.2 multiply_convert_fusion
  316.7 3.2 pad_slice_fusion.8
  322.7 4.4 copy-done.12
  327.1 9.5 %add_convert_fusion = (bf16[5120,128]{1,0:T(8,128)(2,1)}, bf16[5120,128]{1,0:T(8,128)(2,1)S(1)}) fusion(bf16[20,2,2,8,8,128]{5,4,2,3,1,0:T(8,128)(2,1)S(1)} %copy.65, f32[20,2,8,2,8,128]{5,4,3,2,1,0:T(8,128)S(1)} %copy-done.2, bf16[5120,1152]{1,0:T(8,128)(2,1)} %copy-done.12, bf16[1152,128]{1,0:T(8,128)(2,1)S(1)} %bitcast.157), kind=kOutput, calls=%fused_computation.32 | convolution fusion | flops 1518469120 | bytes 18644992 | tf_op jit(solution)/shard_map/dot_general | solution.py:112
  336.6 3.4 pad_slice_fusion
  343.1 3.4 fusion
  346.8 1.0 fusion.1
  347.8 1.1 copy-done.3
  349.0 5.4 convolution_bitcast_fusion
  354.4 9.0 %copy.68 = f32[80,32,8,2,8,2]{0,1,5,4,3,2:T(8,128)} copy(f32[80,32,8,2,8,2]{1,4,5,3,2,0:T(8,128)} %convolution_bitcast_fusion) | data formatting | bytes 5242880 | tf_op jit(solution)/shard_map/transpose | solution.py:23
  363.4 5.1 copy.69
  368.5 3.3 add_convert_fusion.1
  371.7 3.3 gather_fusion.5
  375.1 3.2 broadcast_select_fusion
  378.2 10.5 %all-to-all-start.3 = ((bf16[128,32,256]{2,1,0:T(8,128)(2,1)}), bf16[128,32,256]{2,1,0:T(8,128)(2,1)}, u32[]{:S(2)}, u32[]{:S(2)}) async-start(bf16[128,32,256]{2,1,0:T(8,128)(2,1)} %broadcast_select_fusion), calls=%async_computation.3 | async-start | bytes 4194304 | tf_op jit(solution)/shard_map/all_to_all | solution.py:136
  388.9 1.8 copy.70
  390.9 1.2 convolution_multiply_fusion.2
  392.1 1.2 convolution_multiply_fusion.1
  393.3 7.0 convolution_multiply_fusion
  400.3 86.6 %all-to-all-done.3 = bf16[128,32,256]{2,1,0:T(8,128)(2,1)} async-done(((bf16[128,32,256]{2,1,0:T(8,128)(2,1)}), bf16[128,32,256]{2,1,0:T(8,128)(2,1)}, u32[]{:S(2)}, u32[]{:S(2)}) %all-to-all-start.3) | async-done | bytes 2097184 | tf_op jit(solution)/shard_map/all_to_all | solution.py:136
  486.9 2.4 gather_fusion.6
  489.3 1.3 fusion.3
  490.6 397.9 %all-reduce.5.cloned.1.call-done = (f32[4,32,128]{2,1,0:T(8,128)}, f32[9,128,128]{2,1,0:T(8,128)}, f32[4,32,128]{2,1,0:T(8,128)}) async-done(((f32[4,32,128]{2,1,0:T(8,128)}, f32[9,128,128]{2,1,0:T(8,128)}, f32[4,32,128]{2,1,0:T(8,128)}), (f32[4,32,128]{2,1,0:T(8,128)}, f32[9,128,128]{2,1,0:T(8,128)}, f32[4,32,128]{2,1,0:T(8,128)})) %all-reduce.5.cloned.1.call-update) | async-done | bytes 720912 | tf_op jit(solution)/shard_map/psum | solution.py:139
  888.5 1.5 copy.93
  889.9 1.9 copy.94
  891.9 1.5 copy.95
  (75 shorter events, 9.5 us)
Async XLA Ops:
  7.2 25.2 %copy-start = (bf16[1,80,32,256]{3,2,1,0:T(8,128)(2,1)S(1)}, bf16[1,80,32,256]{3,2,1,0:T(8,128)(2,1)}, u32[]{:S(2)}) copy-start(bf16[1,80,32,256]{3,2,1,0:T(8,128)(2,1)} %param.12) | copy-start | bytes 3932164
  11.7 35.4 %all-to-all-start = ((s32[128,1,1]{2,1,0:T(1,128)}), s32[128,1,1]{2,1,0:T(1,128)S(1)}, u32[]{:S(2)}, u32[]{:S(2)}) async-start(s32[128,1,1]{2,1,0:T(1,128)} %copy.59), calls=%async_computation | async-start | bytes 131072 | tf_op jit(solution)/shard_map/all_to_all | solution.py:96
  32.3 2.0 copy-start.8
  153.2 10.9 %copy-start.10 = (bf16[9,128,128]{2,1,0:T(8,128)(2,1)S(1)}, bf16[9,128,128]{2,1,0:T(8,128)(2,1)}, u32[]{:S(2)}) copy-start(bf16[9,128,128]{2,1,0:T(8,128)(2,1)} %param.18) | copy-start | bytes 884740
  153.2 107.6 %all-to-all-start.1 = ((bf16[128,32,256]{2,1,0:T(8,128)(2,1)}), bf16[128,32,256]{2,1,0:T(8,128)(2,1)S(1)}, u32[]{:S(2)}, u32[]{:S(2)}) async-start(bf16[128,32,256]{2,1,0:T(8,128)(2,1)} %get-tuple-element.38), calls=%async_computation.1 | async-start | bytes 4194304 | tf_op jit(solution)/shard_map/all_to_all | solution.py:95
  279.6 9.7 %copy-start.14 = (bf16[4,32,128]{2,1,0:T(8,128)(2,1)S(1)}, bf16[4,32,128]{2,1,0:T(8,128)(2,1)}, u32[]{:S(2)}) copy-start(bf16[4,32,128]{2,1,0:T(8,128)(2,1)} %param.19) | copy-start | bytes 98308
  303.8 10.4 %copy-start.13 = (bf16[4,32,128]{2,1,0:T(8,128)(2,1)S(1)}, bf16[4,32,128]{2,1,0:T(8,128)(2,1)}, u32[]{:S(2)}) copy-start(bf16[4,32,128]{2,1,0:T(8,128)(2,1)} %param.17) | copy-start | bytes 98308
  322.1 5.0 copy-start.2
  322.1 5.0 copy-start.11
  322.7 4.4 copy-start.12
  336.6 4.6 copy-start.6
  342.1 1.0 copy-start.9
  347.8 1.2 copy-start.3
  378.2 108.7 %all-to-all-start.3 = ((bf16[128,32,256]{2,1,0:T(8,128)(2,1)}), bf16[128,32,256]{2,1,0:T(8,128)(2,1)}, u32[]{:S(2)}, u32[]{:S(2)}) async-start(bf16[128,32,256]{2,1,0:T(8,128)(2,1)} %broadcast_select_fusion), calls=%async_computation.3 | async-start | bytes 4194304 | tf_op jit(solution)/shard_map/all_to_all | solution.py:136
  388.8 1.9 copy-start.4
  388.8 499.7 %all-reduce.5.cloned.1.call-start = ((), (), s32[]{:S(2)}) async-start(), calls=%async_computation.4 | async-start | bytes 1441792 | tf_op jit(solution)/shard_map/psum | solution.py:139
  388.8 2.1 copy-start.5
  390.9 2.4 copy-start.7
  486.9 406.4 %copy-start.1 = (bf16[1,80,32,256]{3,2,1,0:T(8,128)(2,1)S(1)}, bf16[1,80,32,256]{3,2,1,0:T(8,128)(2,1)}, u32[]{:S(2)}) copy-start(bf16[1,80,32,256]{3,2,1,0:T(8,128)(2,1)} %param.12) | copy-start | bytes 3932164
Sparse Core Ops, SparseCore 0:
  400.4 487.9 all-reduce.4
where the time goes:
time: 907 us; the launch traced here: 900 us
  waiting for transfers between devices  581 us (64%)
  local copies, waits for them, and re-layouts  106 us (12%)
  blocking collectives  106 us (12%)
  starting transfers between devices  42 us (5%)
  matrix products  30.3 us (3%)
  other arithmetic  19.5 us (2%)
  between operations  15.6 us (2%)
    psum x1, waiting for transfers between devices, shards(): lax.psum((grad_down * grad_scale, grad_mid * grad_scale, grad_up * grad_s...  398 us
    all_to_all x1, blocking collectives, shards(): lax.all_to_all(lead_send, 'tile', split_axis=0, concat_axis=0, tiled=True)  106 us
    all_to_all x1, waiting for transfers between devices, shards(): lax.all_to_all(cot_send, 'tile', split_axis=0, concat_axis=0, tiled=True)  89.8 us
    all_to_all x1, waiting for transfers between devices, shards(): lax.all_to_all(to_return, 'tile', split_axis=0, concat_axis=0, tiled=True)  86.6 us
    transpose x2, local copies, waits for them, and re-layouts, split_taps(): return blocks.transpose(0, 2, 4, 3, 5, 1).reshape(number, 64, 4 * channels)  20.7 us
    all_to_all x1, starting transfers between devices, shards(): lax.all_to_all(cell_tags, 'tile', split_axis=0, concat_axis=0, tiled=True)  20.6 us
  transfers between devices with their start and end apart: 4, of which 4 were waited for; matrix products, arithmetic and copies ran while one was open for 3% of the time, Pallas kernels for 0%

commit v1 on v0

v1 whole, which is shorter than its diff:
```python
import functools
import math

import jax
import jax.numpy as jnp
from jax import lax
from jax.experimental import pallas as pl
from jax.experimental.pallas import tpu as pltpu
from jax.sharding import PartitionSpec as P

MESH = pl.DeviceIdType.MESH
F32 = jnp.float32
BF16 = jnp.bfloat16
CHUNK = 8
PIXELS = 64
UP_ROWS = 48
DOWN_ROWS = 32
VMEM_LIMIT = 48 * 1024 * 1024


def mm(a, b):
    return jnp.dot(a, b, preferred_element_type=F32)


def mm_nt(a, b):
    return lax.dot_general(a, b, (((1,), (1,)), ((), ())), preferred_element_type=F32)


def mm_tn(a, b):
    return lax.dot_general(a, b, (((0,), (0,)), ((), ())), preferred_element_type=F32)


def sigmoid(v):
    return 1.0 / (1.0 + jnp.exp(-v))


def slope(v):
    g = sigmoid(v)
    return g * (1.0 + v * (1.0 - g))


def shift8(x, step, fill=None):
    if step == 0:
        return x
    place = lax.broadcasted_iota(jnp.int32, x.shape, 1)
    moved = pltpu.roll(x, 7 if step > 0 else 1, 1)
    outside = place == (7 if step > 0 else 0)
    if fill is None:
        return jnp.where(outside, 0.0, moved)
    return jnp.where(outside, pltpu.roll(fill, 7 if step > 0 else 1, 1), moved)


def write_patches(x, patch_ref, flip):
    number = x.shape[0] // PIXELS
    blocks = x.reshape(number * 8, 8, 128)
    for sx in range(3):
        col_step = 1 - sx if flip else sx - 1
        moved = shift8(blocks, col_step).reshape(number, 8, 8, 128)
        for sy in range(3):
            row_step = 1 - sy if flip else sy - 1
            zero = jnp.zeros((number, 1, 8, 128), F32)
            if row_step > 0:
                value = jnp.concatenate([moved[:, 1:], zero], axis=1)
            elif row_step < 0:
                value = jnp.concatenate([zero, moved[:, :7]], axis=1)
            else:
                value = moved
            tap = 3 * sy + sx
            patch_ref[:, tap * 128 : (tap + 1) * 128] = value.reshape(number * PIXELS, 128).astype(BF16)


def spread_weight(weight_ref, spread_ref):
    spread_ref[...] = jnp.zeros_like(spread_ref)
    for tap in range(4):
        for tile in range(4):
            row = tap * 128 + tile * 32
            spread_ref[row : row + 32, tile * 128 : (tile + 1) * 128] = weight_ref[tap]


def to_lanes(x):
    groups = x.shape[0] // (4 * PIXELS)
    rows = []
    for group in range(groups):
        parts = [
            x[(group * 4 + tile) * PIXELS : (group * 4 + tile + 1) * PIXELS] for tile in range(4)
        ]
        rows.append(jnp.concatenate(parts, axis=1))
    return jnp.concatenate(rows, axis=0)


def to_rows(x):
    groups = x.shape[0] // PIXELS
    parts = []
    for group in range(groups):
        for tile in range(4):
            parts.append(x[group * PIXELS : (group + 1) * PIXELS, tile * 128 : (tile + 1) * 128])
    return jnp.concatenate(parts, axis=0)


def taps_of(select, tiles):
    return mm_nt(select, tiles)


def taps_to_lanes(x):
    groups = x.shape[1] // 128
    rows = []
    for group in range(groups):
        parts = [
            x[tap * PIXELS : (tap + 1) * PIXELS, group * 128 : (group + 1) * 128]
            for tap in range(4)
        ]
        rows.append(jnp.concatenate(parts, axis=1))
    return jnp.concatenate(rows, axis=0)


def lanes_to_taps(x):
    groups = x.shape[0] // PIXELS
    columns = []
    for group in range(groups):
        parts = [
            x[group * PIXELS : (group + 1) * PIXELS, tap * 128 : (tap + 1) * 128]
            for tap in range(4)
        ]
        columns.append(jnp.concatenate(parts, axis=0))
    return jnp.concatenate(columns, axis=1)


def holder_first(
    coarse_dev,
    count_ref,
    parent_ref,
    quad_ref,
    fine_ref,
    cot_ref,
    select_ref,
    down_ref,
    up_ref,
    mid_ref,
    x_ref,
    g_ref,
    pre_ref,
    local_ref,
    grad_out_ref,
    send_ref,
    down_s,
    up_s,
    patch_s,
    act_s,
    out_s,
):
    step = pl.program_id(0)
    base = step * CHUNK
    count = count_ref[0]

    @pl.when(step == 0)
    def _():
        spread_weight(down_ref, down_s)
        spread_weight(up_ref, up_s)
        send_ref[...] = jnp.full(send_ref.shape, -1.0, BF16)

    select = select_ref[...]
    x_taps = taps_to_lanes(taps_of(select, fine_ref[...].reshape(CHUNK * 32, 256)).astype(BF16))
    x_ref[...] = x_taps
    pre = to_rows(mm(x_taps, down_s[...]))
    pre_ref[...] = pre
    act = (pre * sigmoid(pre)).astype(BF16).astype(F32)
    act_s[...] = act
    write_patches(act, patch_s, False)

    g_taps = taps_of(select, cot_ref[...].reshape(CHUNK * 32, 256))
    tile_of = lax.broadcasted_iota(jnp.int32, g_taps.shape, 1) // 32
    g_taps = taps_to_lanes(jnp.where(tile_of + base < count, g_taps, 0.0).astype(BF16))
    g_ref[...] = g_taps
    grad_out = to_rows(mm(g_taps, up_s[...])).astype(BF16)
    grad_out_ref[...] = grad_out
    out_s[...] = grad_out.astype(F32)

    local_ref[...] = mm(patch_s[...], mid_ref[...])

    for tile in range(CHUNK):
        parent = parent_ref[base + tile]
        quad = quad_ref[base + tile]
        owner = parent // coarse_dev
        cell = (parent - owner * coarse_dev) * 4 + quad
        low = quad // 2
        edge_y = (1 - low) * 7
        edge_x = (1 - quad % 2) * 7
        parts = []
        for source in (act_s, local_ref, out_s):
            row = source[pl.ds(pl.multiple_of(tile * PIXELS + 8 * edge_y, 8), 8), :]
            col = source[pl.ds(tile * PIXELS + edge_x, 8, stride=8), :]
            col = jnp.where(low == 1, pltpu.roll(col, 7, 0), col)
            parts += [row, col]
        place = lax.broadcasted_iota(jnp.int32, (8, 128), 0)
        parts[5] = jnp.where(place == 7, cell.astype(F32), parts[5])

        @pl.when(base + tile < count)
        def _():
            send_ref[owner] = jnp.concatenate(parts, axis=0).astype(BF16)


def owner_edges(tag_ref, got_ref, mid_ref, back_ref, send_ref, cross_ref, edge_s, reply_s):
    slots = got_ref.shape[0]
    rows = edge_s.shape[2] - 8
    number = rows // 8
    edge_s[...] = jnp.zeros_like(edge_s)

    def take(slot, carry):
        tag = tag_ref[slot]
        cell = jnp.where(tag < 0, number * 4, tag)
        tile, quad = cell // 4, cell % 4
        block = got_ref[slot].astype(F32)
        for kind in range(6):
            part = block[kind * 8 : (kind + 1) * 8]
            if kind % 2 == 1:
                part = jnp.where(quad >= 2, pltpu.roll(part, 1, 0), part)
            edge_s[kind, quad, pl.ds(pl.multiple_of(tile * 8, 8), 8), :] = part
        return carry

    lax.fori_loop(0, slots, take, 0, unroll=4)

    def edge(kind, quad):
        return edge_s[kind, quad, :rows, :].reshape(number, 8, 128)

    place = lax.broadcasted_iota(jnp.int32, (number, 8, 128), 1)

    def corner(x, at):
        return jnp.broadcast_to(x[:, at : at + 1, :], x.shape)

    def side(parts):
        return jnp.concatenate(
            [part.reshape(rows, 128).astype(BF16) for part in parts], axis=1
        )

    grad_row, grad_col = [], []
    for quad in range(4):
        low, right = quad // 2, quad % 2
        at_y, at_x = 7 - 7 * low, 7 - 7 * right
        across, beyond = edge(0, quad ^ 2), edge(0, quad ^ 3)
        beside = edge(1, quad ^ 1)
        fills = [beyond if right == 1 else None, None, beyond if right == 0 else None]
        sy, sx = 2 - 2 * low, 2 - 2 * right
        patch = side([shift8(across, s - 1, fills[s]) for s in range(3)])
        weight = mid_ref[3 * sy * 128 : (3 * sy + 3) * 128]
        row = mm(patch, weight).reshape(number, 8, 128)
        patch = side([shift8(beside, s - 1) for s in range(3)])
        weight = jnp.concatenate(
            [mid_ref[(3 * s + sx) * 128 : (3 * s + sx + 1) * 128] for s in range(3)], axis=0
        )
        col = mm(patch, weight).reshape(number, 8, 128)
        row_sum = row + jnp.where(place == at_x, corner(col, at_y), 0.0)
        col_sum = col + jnp.where(place == at_y, corner(row, at_x), 0.0)
        reply_s[0, quad, :rows, :] = row_sum.reshape(rows, 128)
        reply_s[1, quad, :rows, :] = jnp.where(place == at_y, 0.0, col).reshape(rows, 128)
        go_row = edge(4, quad)
        go_col = jnp.where(place == at_y, corner(go_row, at_x), edge(5, quad))
        grad_row.append((go_row * slope(edge(2, quad) + row_sum)).astype(BF16).astype(F32))
        grad_col.append((go_col * slope(edge(3, quad) + col_sum)).astype(BF16).astype(F32))

    cross_ref[...] = jnp.zeros_like(cross_ref)
    for quad in range(4):
        low, right = quad // 2, quad % 2
        at_y, at_x = 7 - 7 * low, 7 - 7 * right
        across, beyond, beside = grad_row[quad ^ 2], grad_row[quad ^ 3], grad_col[quad ^ 1]
        sy, sx = 2 * low, 2 * right
        fills = [beyond if right == 0 else None, None, beyond if right == 1 else None]
        patch = side([shift8(across, 1 - s, fills[s]) for s in range(3)])
        row = mm(patch, back_ref[3 * sy * 128 : (3 * sy + 3) * 128]).reshape(number, 8, 128)
        act_row = edge_s[0, quad, :rows, :].astype(BF16)
        cross_ref[:, 3 * sy * 128 : (3 * sy + 3) * 128] += mm_tn(act_row, patch)
        patch = side([shift8(beside, 1 - s) for s in range(3)])
        weight = jnp.concatenate(
            [back_ref[(3 * s + sx) * 128 : (3 * s + sx + 1) * 128] for s in range(3)], axis=0
        )
        col = mm(patch, weight).reshape(number, 8, 128)
        act_col = edge_s[1, quad, :rows, :].astype(BF16)
        part = mm_tn(act_col, patch)
        for s in range(3):
            tap = 3 * s + sx
            cross_ref[:, tap * 128 : (tap + 1) * 128] += part[:, s * 128 : (s + 1) * 128]
        row_sum = row + jnp.where(place == at_x, corner(col, at_y), 0.0)
        reply_s[2, quad, :rows, :] = row_sum.reshape(rows, 128)
        reply_s[3, quad, :rows, :] = jnp.where(place == at_y, 0.0, col).reshape(rows, 128)

    reply_s[:, :, rows:, :] = jnp.zeros((4, 4, 8, 128), F32)

    def give(slot, carry):
        tag = tag_ref[slot]
        cell = jnp.where(tag < 0, number * 4, tag)
        tile, quad = cell // 4, cell % 4
        parts = [
            reply_s[kind, quad, pl.ds(pl.multiple_of(tile * 8, 8), 8), :] for kind in range(4)
        ]
        send_ref[slot] = jnp.concatenate(parts, axis=0).astype(BF16)
        return carry

    lax.fori_loop(0, slots, give, 0, unroll=4)


def holder_last(
    coarse_dev,
    scale,
    count_ref,
    parent_ref,
    quad_ref,
    cot_ref,
    x_ref,
    g_ref,
    pre_ref,
    local_ref,
    grad_out_ref,
    got_ref,
    cross_ref,
    select_ref,
    down_ref,
    back_ref,
    fine_ref,
    weights_ref,
    down_s,
    patch_s,
    mid_s,
    act_s,
    mid_acc,
    down_acc,
    up_acc,
):
    step = pl.program_id(0)
    base = step * CHUNK
    count = count_ref[0]

    @pl.when(step == 0)
    def _():
        spread_weight(down_ref, down_s)
        mid_acc[...] = cross_ref[...]
        down_acc[...] = jnp.zeros_like(down_acc)
        up_acc[...] = jnp.zeros_like(up_acc)

    def add_edges(target, first):
        for tile in range(CHUNK):

            @pl.when(base + tile < count)
            def _():
                owner = parent_ref[base + tile] // coarse_dev
                quad = quad_ref[base + tile]
                edge_y = (1 - quad // 2) * 7
                edge_x = (1 - quad % 2) * 7
                block = got_ref[owner, first : first + 16, :].astype(F32)
                at_row = pl.ds(pl.multiple_of(tile * PIXELS + 8 * edge_y, 8), 8)
                target[at_row, :] += block[:8]
                at_col = pl.ds(tile * PIXELS + edge_x, 8, stride=8)
                target[at_col, :] += block[8:]

    mid_s[...] = local_ref[...]
    add_edges(mid_s, 0)
    mid = mid_s[...]
    gate = sigmoid(mid)
    pre = pre_ref[...]
    pre_gate = sigmoid(pre)
    act = (pre * pre_gate).astype(BF16)
    out = (act.astype(F32) + mid * gate).astype(BF16)
    grad_out = grad_out_ref[...].astype(F32)
    grad_mid_pre = (grad_out * (gate * (1.0 + mid * (1.0 - gate)))).astype(BF16)
    write_patches(grad_mid_pre.astype(F32), patch_s, True)
    act_s[...] = grad_out + mm(patch_s[...], back_ref[...])
    add_edges(act_s, 16)
    mid_acc[...] += mm_tn(act, patch_s[...])
    up_acc[...] += mm_tn(g_ref[...], to_lanes(out))
    grad_act = act_s[...].astype(BF16).astype(F32)
    grad_pre = (grad_act * (pre_gate * (1.0 + pre * (1.0 - pre_gate)))).astype(BF16)
    grad_pre = to_lanes(grad_pre)
    down_acc[...] += mm_tn(x_ref[...], grad_pre)
    back = lanes_to_taps(mm_nt(grad_pre, down_s[...]))
    high = back.astype(BF16)
    rest = (back - high.astype(F32)).astype(BF16)
    select = select_ref[...]
    fine_back = mm_tn(high, select) + mm_tn(rest, select)
    total = cot_ref[...].reshape(CHUNK * 32, 256).astype(F32) + fine_back
    tile_of = lax.broadcasted_iota(jnp.int32, total.shape, 0) // 32
    total = jnp.where(tile_of + base < count, total, 0.0)
    fine_ref[...] = total.astype(BF16).reshape(CHUNK, 32, 256)

    @pl.when(step == pl.num_programs(0) - 1)
    def _():
        for tap in range(9):
            weights_ref[tap * 128 : (tap + 1) * 128, :] = (
                mid_acc[:, tap * 128 : (tap + 1) * 128] * scale
            ).astype(BF16)
        for index, acc in enumerate((down_acc, up_acc)):
            for tap in range(4):
                part = jnp.zeros((32, 128), F32)
                for tile in range(4):
                    row = tap * 128 + tile * 32
                    part += acc[row : row + 32, tile * 128 : (tile + 1) * 128]
                row = 1152 + index * 128 + tap * 32
                weights_ref[row : row + 32, :] = (part * scale).astype(BF16)
        weights_ref[1408:, :] = jnp.zeros((weights_ref.shape[0] - 1408, 128), BF16)


def sum_weights(
    events, plane, depth, pieces, mine_ref, total_ref, near_s, sum_s, far_s, fin_s, low_s, all_s,
    near_send, near_recv, far_send, far_recv, fin_send, fin_recv, all_send, all_recv,
):
    event = lax.axis_index("event")
    tile = lax.axis_index("tile")
    z = tile // plane
    low = tile % plane
    group = events * plane
    me = event * plane + low
    share = mine_ref.shape[0] // group
    piece = share // pieces

    def near_id(p):
        return (p // plane, z * plane + p % plane)

    def far_id(p):
        return (event, p * plane + low)

    barrier = pltpu.get_barrier_semaphore()

    def greet_near(k, carry):
        pl.semaphore_signal(
            barrier, inc=1, device_id=near_id((me + k) % group), device_id_type=MESH
        )
        return carry

    def greet_far(k, carry):
        pl.semaphore_signal(
            barrier, inc=1, device_id=far_id((z + k) % depth), device_id_type=MESH
        )
        return carry

    lax.fori_loop(1, group, greet_near, 0)
    lax.fori_loop(1, depth, greet_far, 0)
    pl.semaphore_wait(barrier, group + depth - 2)

    def rows(p):
        return pl.ds(pl.multiple_of(p * share, 16), share)

    def near_copy(to, slot):
        return pltpu.make_async_remote_copy(
            src_ref=mine_ref.at[rows(to)],
            dst_ref=near_s.at[slot],
            send_sem=near_send.at[to],
            recv_sem=near_recv.at[slot],
            device_id=near_id(to),
            device_id_type=MESH,
        )

    def send_near(k, carry):
        near_copy((me + k) % group, me).start()
        return carry

    lax.fori_loop(1, group, send_near, 0)

    def take_near(k, total):
        p = (me + k) % group
        near_copy(p, p).wait_recv()
        return total + near_s[p].astype(F32)

    total = lax.fori_loop(1, group, take_near, mine_ref[rows(me), :].astype(F32))
    sum_s[...] = total.reshape(pieces, piece, 128)

    def far_copy(to, slot):
        return pltpu.make_async_remote_copy(
            src_ref=sum_s.at[to],
            dst_ref=far_s.at[slot],
            send_sem=far_send.at[to],
            recv_sem=far_recv.at[slot],
            device_id=far_id(to),
            device_id_type=MESH,
        )

    for to in range(pieces):

        @pl.when(z != to)
        def _():
            far_copy(to, z).start()

    def fin_copy(to, slot):
        return pltpu.make_async_remote_copy(
            src_ref=fin_s.at[slot],
            dst_ref=fin_s.at[slot],
            send_sem=fin_send.at[to],
            recv_sem=fin_recv.at[slot],
            device_id=far_id(to),
            device_id_type=MESH,
        )

    @pl.when(z < pieces)
    def _():
        def take_far(k, total):
            p = (z + k) % depth
            far_copy(z, p).wait_recv()
            return total + far_s[p]

        fin_s[z] = lax.fori_loop(1, depth, take_far, sum_s[z])

        def send_fin(k, carry):
            fin_copy((z + k) % depth, z).start()
            return carry

        lax.fori_loop(1, depth, send_fin, 0)

    for p in range(pieces):

        @pl.when(z != p)
        def _():
            fin_copy(p, p).wait_recv()

    low_s[...] = fin_s[...].reshape(share, 128).astype(BF16)

    def all_copy(to, slot):
        return pltpu.make_async_remote_copy(
            src_ref=low_s,
            dst_ref=all_s.at[rows(slot)],
            send_sem=all_send.at[to],
            recv_sem=all_recv.at[slot],
            device_id=near_id(to),
            device_id_type=MESH,
        )

    def send_all(k, carry):
        all_copy((me + k) % group, me).start()
        return carry

    lax.fori_loop(1, group, send_all, 0)
    all_s[rows(me), :] = low_s[...]

    def take_all(k, carry):
        p = (me + k) % group
        all_copy(p, p).wait_recv()
        return carry

    lax.fori_loop(1, group, take_all, 0)
    total_ref[...] = all_s[...].astype(F32)

    def sent_near(k, carry):
        p = (me + k) % group
        near_copy(p, me).wait_send()
        all_copy(p, me).wait_send()
        return carry

    lax.fori_loop(1, group, sent_near, 0)
    for to in range(pieces):

        @pl.when(z != to)
        def _():
            far_copy(to, z).wait_send()

    @pl.when(z < pieces)
    def _():
        def sent_fin(k, carry):
            fin_copy((z + k) % depth, z).wait_send()
            return carry

        lax.fori_loop(1, depth, sent_fin, 0)


def full(shape):
    return pl.BlockSpec(shape, lambda *_: (0,) * len(shape))


def chunked(shape):
    return pl.BlockSpec(shape, lambda step, *_: (step,) + (0,) * (len(shape) - 1))


def fine_select():
    row = lax.broadcasted_iota(jnp.int32, (256, 256), 0)
    column = lax.broadcasted_iota(jnp.int32, (256, 256), 1)
    tap, i, j = row // 64, row // 8 % 8, row % 8
    return (column == 16 * (2 * i + tap // 2) + 2 * j + tap % 2).astype(BF16)


def shards(plane, fine, cotangent, counts, parent, quadrant, down_weight, mid_weight, up_weight):
    number = fine.shape[1]
    slots = lax.axis_size("tile")
    events = lax.axis_size("event")
    coarse_dev = number // 4
    rows = number * PIXELS
    steps = number // CHUNK
    step_rows = CHUNK * PIXELS
    scale = 1.0 / math.sqrt(events * slots * number * 64)
    select = fine_select()
    mid_flat = mid_weight.reshape(9 * 128, 128)
    mid_back = jnp.transpose(mid_weight, (0, 2, 1)).reshape(9 * 128, 128)
    scalars = (counts[0], parent[0], quadrant[0])
    fine_tiles, cot_tiles = fine[0], cotangent[0]

    x_taps, g_taps, pre, local, grad_out, up = pl.pallas_call(
        functools.partial(holder_first, coarse_dev),
        grid_spec=pltpu.PrefetchScalarGridSpec(
            num_scalar_prefetch=3,
            grid=(steps,),
            in_specs=[
                chunked((CHUNK, 32, 256)),
                chunked((CHUNK, 32, 256)),
                full((256, 256)),
                full((4, 32, 128)),
                full((4, 32, 128)),
                full((1152, 128)),
            ],
            out_specs=[
                chunked((step_rows // 4, 512)),
                chunked((step_rows // 4, 512)),
                chunked((step_rows, 128)),
                chunked((step_rows, 128)),
                chunked((step_rows, 128)),
                full((slots, UP_ROWS, 128)),
            ],
            scratch_shapes=[
                pltpu.VMEM((512, 512), BF16),
                pltpu.VMEM((512, 512), BF16),
                pltpu.VMEM((step_rows, 1152), BF16),
                pltpu.VMEM((step_rows, 128), F32),
                pltpu.VMEM((step_rows, 128), F32),
            ],
        ),
        out_shape=[
            jax.ShapeDtypeStruct((rows // 4, 512), BF16),
            jax.ShapeDtypeStruct((rows // 4, 512), BF16),
            jax.ShapeDtypeStruct((rows, 128), F32),
            jax.ShapeDtypeStruct((rows, 128), F32),
            jax.ShapeDtypeStruct((rows, 128), BF16),
            jax.ShapeDtypeStruct((slots, UP_ROWS, 128), BF16),
        ],
        compiler_params=pltpu.CompilerParams(vmem_limit_bytes=VMEM_LIMIT),
        name="holder_first",
    )(*scalars, fine_tiles, cot_tiles, select, down_weight, up_weight, mid_flat)

    got = lax.all_to_all(up, "tile", split_axis=0, concat_axis=0, tiled=True)
    tags = got[:, UP_ROWS - 1, 0].astype(jnp.int32)
    smem = pl.BlockSpec(memory_space=pltpu.SMEM)
    vmem = pl.BlockSpec(memory_space=pltpu.VMEM)
    reply, cross = pl.pallas_call(
        owner_edges,
        in_specs=[smem, vmem, vmem, vmem],
        out_specs=[vmem, vmem],
        out_shape=[
            jax.ShapeDtypeStruct((slots, DOWN_ROWS, 128), BF16),
            jax.ShapeDtypeStruct((128, 1152), F32),
        ],
        scratch_shapes=[
            pltpu.VMEM((6, 4, coarse_dev * 8 + 8, 128), F32),
            pltpu.VMEM((4, 4, coarse_dev * 8 + 8, 128), F32),
        ],
        compiler_params=pltpu.CompilerParams(vmem_limit_bytes=VMEM_LIMIT),
        name="owner_edges",
    )(tags, got, mid_flat, mid_back)
    back = lax.all_to_all(reply, "tile", split_axis=0, concat_axis=0, tiled=True)

    group = events * plane
    share = -(-1408 // (group * 16)) * 16
    grad_fine, weights = pl.pallas_call(
        functools.partial(holder_last, coarse_dev, scale),
        grid_spec=pltpu.PrefetchScalarGridSpec(
            num_scalar_prefetch=3,
            grid=(steps,),
            in_specs=[
                chunked((CHUNK, 32, 256)),
                chunked((step_rows // 4, 512)),
                chunked((step_rows // 4, 512)),
                chunked((step_rows, 128)),
                chunked((step_rows, 128)),
                chunked((step_rows, 128)),
                full((slots, DOWN_ROWS, 128)),
                full((128, 1152)),
                full((256, 256)),
                full((4, 32, 128)),
                full((1152, 128)),
            ],
            out_specs=[chunked((CHUNK, 32, 256)), full((group * share, 128))],
            scratch_shapes=[
                pltpu.VMEM((512, 512), BF16),
                pltpu.VMEM((step_rows, 1152), BF16),
                pltpu.VMEM((step_rows, 128), F32),
                pltpu.VMEM((step_rows, 128), F32),
                pltpu.VMEM((128, 1152), F32),
                pltpu.VMEM((512, 512), F32),
                pltpu.VMEM((512, 512), F32),
            ],
        ),
        out_shape=[
            jax.ShapeDtypeStruct((number, 32, 256), BF16),
            jax.ShapeDtypeStruct((group * share, 128), BF16),
        ],
        compiler_params=pltpu.CompilerParams(vmem_limit_bytes=VMEM_LIMIT),
        name="holder_last",
    )(
        *scalars, cot_tiles, x_taps, g_taps, pre, local, grad_out, back, cross, select,
        down_weight, mid_back,
    )

    depth = slots // plane
    pieces = max(n for n in range(1, share // 8 + 1) if share // 8 % n == 0 and n <= depth)
    piece = share // pieces
    dma = pltpu.SemaphoreType.DMA
    total = pl.pallas_call(
        functools.partial(sum_weights, events, plane, depth, pieces),
        in_specs=[vmem],
        out_specs=vmem,
        out_shape=jax.ShapeDtypeStruct((group * share, 128), F32),
        scratch_shapes=[
            pltpu.VMEM((group, share, 128), BF16),
            pltpu.VMEM((pieces, piece, 128), F32),
            pltpu.VMEM((depth, piece, 128), F32),
            pltpu.VMEM((pieces, piece, 128), F32),
            pltpu.VMEM((share, 128), BF16),
            pltpu.VMEM((group * share, 128), BF16),
            dma((group,)),
            dma((group,)),
            dma((pieces,)),
            dma((depth,)),
            dma((depth,)),
            dma((pieces,)),
            dma((group,)),
            dma((group,)),
        ],
        compiler_params=pltpu.CompilerParams(
            collective_id=0, has_side_effects=True, vmem_limit_bytes=VMEM_LIMIT
        ),
        name="sum_weights",
    )(weights)
    return (
        grad_fine[None],
        total[1152:1280].reshape(4, 32, 128),
        total[:1152].reshape(9, 128, 128),
        total[1280:1408].reshape(4, 32, 128),
    )


def solution(mesh):
    placed = (
        P("event", "tile", None, None),
        P("event", "tile", None, None),
        P("event", "tile"),
        P("event", "tile"),
        P("event", "tile"),
        P(),
        P(),
        P(),
    )
    return jax.shard_map(
        functools.partial(shards, 8),
        mesh=mesh,
        in_specs=placed,
        out_specs=(P("event", "tile", None, None), P(), P(), P()),
        check_vma=False,
    )
```

time: 907 us -> 257 us (0.28)
  waiting for transfers between devices: 581 us -> 73.5 us
  local copies, waits for them, and re-layouts: 106 us -> 9.14 us
  Pallas kernels: 0 us -> 85.9 us
  blocking collectives: 106 us -> 62.7 us
  matrix products: 30.3 us -> 0 us
  starting transfers between devices: 42 us -> 20.7 us
  other arithmetic: 19.5 us -> 2.94 us
  between operations: 15.6 us -> 1.45 us
    psum x1 -> x0, waiting for transfers between devices: 398 us -> none  [shards(): lax.psum((grad_down * grad_scale, grad_mid * grad_scale, grad_up * grad_s...]
    all_to_all x3 -> x1, waiting for transfers between devices: 183 us -> 73.5 us  [shards(): got = lax.all_to_all(up, 'tile', split_axis=0, concat_axis=0, tiled=True)]
    pallas_call x0 -> x4, Pallas kernels: none -> 85.9 us  [the longest x1 39 us: shards(): pl.pallas_call(functools.partial(sum_weights, events, plane, depth, piece...]
    all_to_all x1, blocking collectives: 106 us -> 62.7 us  [shards(): lax.all_to_all(reply, 'tile', split_axis=0, concat_axis=0, tiled=True)]
    dot_general x8 -> x0, matrix products: 30.3 us -> none  [the longest x1 9.46 us: shards(): mid_pre = jnp.dot(act_patch, mid_flat, preferred_element_type=jnp.float32)]
    transpose x3 -> x1, local copies, waits for them, and re-layouts: 29.7 us -> 0.22 us  [shards(): mid_back = jnp.transpose(mid_weight, (0, 2, 1)).reshape(9 * 128, 128)]
    another operation x4 -> x0, local copies, waits for them, and re-layouts: 22.2 us -> none  [the longest x1 10.4 us: shards(): child_taps = split_taps(lead_quads).reshape(-1, 4 * fine_ch)]
    all_to_all x3 -> x1, starting transfers between devices: 41.9 us -> 20.7 us  [shards(): got = lax.all_to_all(up, 'tile', split_axis=0, concat_axis=0, tiled=True)]
  transfers between devices with their start and end apart: 4 -> 1, of which waited for: 4 -> 1; matrix products, arithmetic and copies ran while one was open for 3% -> 0% of each run, Pallas kernels for 0% -> 0%
where the time goes in v1:
time: 257 us; the launch traced here: 256 us
  Pallas kernels  85.9 us (33%)
  waiting for transfers between devices  73.5 us (29%)
  blocking collectives  62.7 us (24%)
  starting transfers between devices  20.7 us (8%)
  local copies, waits for them, and re-layouts  9.14 us (4%)
  other arithmetic  2.94 us (1%)
    all_to_all x1, waiting for transfers between devices, shards(): got = lax.all_to_all(up, 'tile', split_axis=0, concat_axis=0, tiled=True)  73.5 us
    all_to_all x1, blocking collectives, shards(): lax.all_to_all(reply, 'tile', split_axis=0, concat_axis=0, tiled=True)  62.7 us
    pallas_call x1, Pallas kernels, shards(): pl.pallas_call(functools.partial(sum_weights, events, plane, depth, piece...  39 us
    pallas_call x1, Pallas kernels, shards(): pl.pallas_call(functools.partial(holder_last, coarse_dev, scale), grid_sp...  27.3 us
    all_to_all x1, starting transfers between devices, shards(): got = lax.all_to_all(up, 'tile', split_axis=0, concat_axis=0, tiled=True)  20.7 us
    pallas_call x1, Pallas kernels, shards(): pl.pallas_call(functools.partial(holder_first, coarse_dev), grid_spec=plt...  15.2 us
    unnamed x30, local copies, waits for them, and re-layouts  7.41 us
  transfers between devices with their start and end apart: 1, of which 1 were waited for; matrix products, arithmetic and copies ran while one was open for 0% of the time, Pallas kernels for 0%

profile of v1, /device:TPU:1, one launch (start us, length us, event | category | flops | bytes accessed | tf_op | source)
XLA Modules:
  0.0 256.3 jit_solution(8510098006055316685)
XLA Ops:
  1.3 0.6 fusion.11.select_ref
  1.9 0.0 copy-start.6
  1.9 0.0 copy-start.1
  1.9 1.0 copy-done.1
  2.9 0.0 copy-start.3
  2.9 1.3 copy-done.3
  4.2 0.0 copy-start.8
  4.2 0.8 copy-done.8
  5.0 0.0 copy-start.10
  5.0 0.8 copy-done.10
  5.8 0.0 copy-start.11
  5.8 0.7 copy-done.11
  6.4 0.0 copy-start.13
  6.4 0.7 copy-done.13
  7.1 15.2 %holder_first.1 = (bf16[1280,512]{1,0:T(8,128)(2,1)S(1)}, bf16[1280,512]{1,0:T(8,128)(2,1)S(1)}, f32[5120,128]{1,0:T(8,128)}, f32[5120,128]{1,0:T(8,128)}, bf16[...) custom-call(s32[1]{0:T(128)} %bitcast.12.count_ref, s32[80]{0:T(128)S(1)} %bitcast.22, s32[80]{0:T(128)S(1)} %bitcast.24, ...), custom_call_target="tpu_custom_call" | custom-call | tf_op jit(solution)/shard_map/holder_first/pallas_call | solution.py:589
  22.3 0.0 copy-done.6
  22.3 0.0 copy-start.4
  22.3 1.1 copy-done.4
  23.4 0.0 copy-start.5
  23.4 1.1 copy-done.5
  24.6 0.0 copy-start.2
  24.6 20.7 %all-to-all-start = ((bf16[128,48,128]{2,1,0:T(8,128)(2,1)}), bf16[128,48,128]{2,1,0:T(8,128)(2,1)S(1)}, u32[]{:S(2)}, u32[]{:S(2)}) async-start(bf16[128,48,128]{2,1,0:T(8,128)(2,1)} %get-tuple-element.19), calls=%async_computation | async-start | bytes 3145728 | tf_op jit(solution)/shard_map/all_to_all | solution.py:630
  45.3 0.0 copy-done.2
  45.3 0.2 copy.13
  45.5 73.5 %all-to-all-done.got_ref = bf16[128,48,128]{2,1,0:T(8,128)(2,1)S(1)} async-done(((bf16[128,48,128]{2,1,0:T(8,128)(2,1)}), bf16[128,48,128]{2,1,0:T(8,128)(2,1)S(1)}, u32[]{:S(2)}, u32[]{:S(2)}) %all-to-all-start) | async-done | bytes 1572896 | tf_op jit(solution)/shard_map/all_to_all | solution.py:630
  119.0 2.4 fusion.12.tag_ref
  121.3 4.4 %owner_edges.1 = (bf16[128,32,128]{2,1,0:T(8,128)(2,1)S(1)}, f32[128,1152]{1,0:T(8,128)S(1)}) custom-call(s32[128]{0:T(128)S(1)} %fusion.12.tag_ref, bf16[128,48,128]{2,1,0:T(8,128)(2,1)S(1)} %all-to-all-done.got_ref, bf16[1152,128]{1,0:T(8,128)(2,1)S(1)} %bitcast.18, bf16[1152,128]{1,0:T(8,128)(2,1)S(1)} %bitcast.19), custom_call_target="tpu_custom_call" | custom-call | tf_op jit(solution)/shard_map/owner_edges/pallas_call | solution.py:634
  125.7 0.0 copy-start
  125.7 0.0 copy-start.7
  125.7 0.0 copy-start.9
  125.7 0.0 copy-start.12
  125.7 0.0 copy-start.14
  125.8 62.7 %all_to_all.10.got_ref = bf16[128,32,128]{2,1,0:T(8,128)(2,1)S(1)} all-to-all(bf16[128,32,128]{2,1,0:T(8,128)(2,1)S(1)} %get-tuple-element.20), channel_id=1, replica_groups=mesh['event'=4,'tile'=128] {'tile'}, dimensions={0} | all-to-all | bytes 2097152 | tf_op jit(solution)/shard_map/all_to_all | solution.py:649
  188.4 0.0 copy-done
  188.4 0.0 copy-done.7
  188.4 0.0 copy-done.9
  188.4 0.0 copy-done.12
  188.4 0.0 copy-done.14
  188.4 27.3 %holder_last.1 = (bf16[80,32,256]{2,1,0:T(8,128)(2,1)}, bf16[1536,128]{1,0:T(8,128)(2,1)S(1)}) custom-call(s32[1]{0:T(128)} %bitcast.13.count_ref, s32[80]{0:T(128)S(1)} %bitcast.23, s32[80]{0:T(128)S(1)} %bitcast.25, bf16[80,32,256]{2,1,0:T(8,128)(2,1)S(1)} %bitcast.15, bf16[1280,512]{1,0:T(8,128)(2,1)S(1)} %get-tuple-element.14.x_ref, ...), custom_call_target="tpu_custom_call" | custom-call | tf_op jit(solution)/shard_map/holder_last/pallas_call | solution.py:653
  215.7 39.0 %sum_weights.1 = f32[1536,128]{1,0:T(8,128)S(1)} custom-call(bf16[1536,128]{1,0:T(8,128)(2,1)S(1)} %get-tuple-element.23.mine_ref), custom_call_target="tpu_custom_call" | custom-call | tf_op jit(solution)/shard_map/sum_weights/pallas_call | solution.py:697
  254.8 0.7 fusion.17
  255.4 0.9 slice.14
  (5 shorter events, 0.0 us)
Async XLA Ops:
  1.9 20.4 %copy-start.6 = (bf16[256,256]{1,0:T(8,128)(2,1)}, bf16[256,256]{1,0:T(8,128)(2,1)S(1)}, u32[]{:S(2)}) copy-start(bf16[256,256]{1,0:T(8,128)(2,1)S(1)} %fusion.11.select_ref) | copy-start | bytes 393220
  1.9 1.0 copy-start.1
  2.9 1.3 copy-start.3
  4.2 0.8 copy-start.8
  5.0 0.8 copy-start.10
  5.8 0.7 copy-start.11
  6.4 0.7 copy-start.13
  22.3 1.1 copy-start.4
  23.4 1.1 copy-start.5
  24.6 20.7 %copy-start.2 = (bf16[9,128,128]{2,1,0:T(8,128)(2,1)S(1)}, bf16[9,128,128]{2,1,0:T(8,128)(2,1)}, u32[]{:S(2)}) copy-start(bf16[9,128,128]{2,1,0:T(8,128)(2,1)} %param.14) | copy-start | bytes 884740
  24.6 94.4 %all-to-all-start = ((bf16[128,48,128]{2,1,0:T(8,128)(2,1)}), bf16[128,48,128]{2,1,0:T(8,128)(2,1)S(1)}, u32[]{:S(2)}, u32[]{:S(2)}) async-start(bf16[128,48,128]{2,1,0:T(8,128)(2,1)} %get-tuple-element.19), calls=%async_computation | async-start | bytes 3145728 | tf_op jit(solution)/shard_map/all_to_all | solution.py:630
  125.7 62.7 %copy-start = (bf16[1,80,32,256]{3,2,1,0:T(8,128)(2,1)S(1)}, bf16[1,80,32,256]{3,2,1,0:T(8,128)(2,1)}, u32[]{:S(2)}) copy-start(bf16[1,80,32,256]{3,2,1,0:T(8,128)(2,1)} %param.9) | copy-start | bytes 3932164
  125.7 62.7 %copy-start.7 = (bf16[256,256]{1,0:T(8,128)(2,1)S(1)}, bf16[256,256]{1,0:T(8,128)(2,1)}, u32[]{:S(2)}) copy-start(bf16[256,256]{1,0:T(8,128)(2,1)} %copy-done.6) | copy-start | bytes 393220
  125.7 62.7 %copy-start.9 = (bf16[4,32,128]{2,1,0:T(8,128)(2,1)S(1)}, bf16[4,32,128]{2,1,0:T(8,128)(2,1)}, u32[]{:S(2)}) copy-start(bf16[4,32,128]{2,1,0:T(8,128)(2,1)} %down_ref.3) | copy-start | bytes 98308
  125.7 62.7 %copy-start.12 = (s32[1,80]{1,0:T(1,128)S(1)}, s32[1,80]{1,0:T(1,128)}, u32[]{:S(2)}) copy-start(s32[1,80]{1,0:T(1,128)} %param.11) | copy-start | bytes 964
  125.7 62.7 %copy-start.14 = (s32[1,80]{1,0:T(1,128)S(1)}, s32[1,80]{1,0:T(1,128)}, u32[]{:S(2)}) copy-start(s32[1,80]{1,0:T(1,128)} %param.12) | copy-start | bytes 964

commit v2 on v1

v2 whole, which is shorter than its diff:
```python
import functools
import math

import jax
import jax.numpy as jnp
from jax import lax
from jax.experimental import pallas as pl
from jax.experimental.pallas import tpu as pltpu
from jax.sharding import PartitionSpec as P

MESH = pl.DeviceIdType.MESH
F32 = jnp.float32
BF16 = jnp.bfloat16
CHUNK = 16
PIXELS = 64
EDGE_ROWS = 16
VMEM_LIMIT = 48 * 1024 * 1024
FIRST_LIMIT = 60 * 1024 * 1024


def mm(a, b):
    return jnp.dot(a, b, preferred_element_type=F32)


def mm_nt(a, b):
    return lax.dot_general(a, b, (((1,), (1,)), ((), ())), preferred_element_type=F32)


def mm_tn(a, b):
    return lax.dot_general(a, b, (((0,), (0,)), ((), ())), preferred_element_type=F32)


def sigmoid(v):
    return 0.5 * jnp.tanh(0.5 * v) + 0.5


def slope(v):
    g = sigmoid(v)
    return g * (1.0 + v * (1.0 - g))


def shift8(x, step, fill=None):
    if step == 0:
        return x
    place = lax.broadcasted_iota(jnp.int32, x.shape, 1)
    moved = pltpu.roll(x, 7 if step > 0 else 1, 1)
    outside = place == (7 if step > 0 else 0)
    if fill is None:
        return jnp.where(outside, 0.0, moved)
    return jnp.where(outside, pltpu.roll(fill, 7 if step > 0 else 1, 1), moved)


def side_steps(x, flip):
    blocks = x.reshape(x.shape[0] // 8, 8, 128)
    parts = [shift8(blocks, 1 - s if flip else s - 1) for s in range(3)]
    return jnp.concatenate([part.reshape(x.shape).astype(BF16) for part in parts], axis=1)


def row_step(x, step):
    if step == 0:
        return x
    blocks = x.reshape(x.shape[0] // PIXELS, 8, 8, 128)
    zero = jnp.zeros((blocks.shape[0], 1, 8, 128), x.dtype)
    if step > 0:
        moved = jnp.concatenate([blocks[:, 1:], zero], axis=1)
    else:
        moved = jnp.concatenate([zero, blocks[:, :7]], axis=1)
    return moved.reshape(x.shape)


def spread_weight(weight_ref, spread_ref):
    spread_ref[...] = jnp.zeros_like(spread_ref)
    for tap in range(4):
        for tile in range(4):
            row = tap * 128 + tile * 32
            spread_ref[row : row + 32, tile * 128 : (tile + 1) * 128] = weight_ref[tap]


def to_lanes(x):
    groups = x.shape[0] // (4 * PIXELS)
    rows = []
    for group in range(groups):
        parts = [
            x[(group * 4 + tile) * PIXELS : (group * 4 + tile + 1) * PIXELS] for tile in range(4)
        ]
        rows.append(jnp.concatenate(parts, axis=1))
    return jnp.concatenate(rows, axis=0)


def to_rows(x):
    groups = x.shape[0] // PIXELS
    parts = []
    for group in range(groups):
        for tile in range(4):
            parts.append(x[group * PIXELS : (group + 1) * PIXELS, tile * 128 : (tile + 1) * 128])
    return jnp.concatenate(parts, axis=0)


def taps_to_lanes(x):
    groups = x.shape[1] // 128
    rows = []
    for group in range(groups):
        parts = [
            x[tap * PIXELS : (tap + 1) * PIXELS, group * 128 : (group + 1) * 128]
            for tap in range(4)
        ]
        rows.append(jnp.concatenate(parts, axis=1))
    return jnp.concatenate(rows, axis=0)


def lanes_to_taps(x):
    groups = x.shape[0] // PIXELS
    columns = []
    for group in range(groups):
        parts = [
            x[group * PIXELS : (group + 1) * PIXELS, tap * 128 : (tap + 1) * 128]
            for tap in range(4)
        ]
        columns.append(jnp.concatenate(parts, axis=0))
    return jnp.concatenate(columns, axis=1)


def fill_select(select_s):
    row = lax.broadcasted_iota(jnp.int32, (256, 256), 0)
    column = lax.broadcasted_iota(jnp.int32, (256, 256), 1)
    tap, i, j = row // 64, row // 8 % 8, row % 8
    meet = column == 16 * (2 * i + tap // 2) + 2 * j + tap % 2
    select_s[...] = jnp.where(meet, 1.0, 0.0).astype(BF16)


def place_of(quad):
    return (1 - quad // 2) * 7, (1 - quad % 2) * 7


def read_edges(source, tile, quad):
    edge_y, edge_x = place_of(quad)
    row = source[pl.ds(pl.multiple_of(tile * PIXELS + 8 * edge_y, 8), 8), :]
    col = source[pl.ds(tile * PIXELS + edge_x, 8, stride=8), :]
    return row, jnp.where(quad >= 2, pltpu.roll(col, 7, 0), col)


def add_edges(target, got_ref, base, coarse_dev, count, parent_ref, quad_ref):
    for tile in range(CHUNK):

        @pl.when(base + tile < count)
        def _():
            owner = parent_ref[base + tile] // coarse_dev
            edge_y, edge_x = place_of(quad_ref[base + tile])
            block = got_ref[owner].astype(F32)
            at_row = pl.ds(pl.multiple_of(tile * PIXELS + 8 * edge_y, 8), 8)
            target[at_row, :] += block[:8]
            at_col = pl.ds(tile * PIXELS + edge_x, 8, stride=8)
            target[at_col, :] += block[8:]


def down_conv(
    coarse_dev, count_ref, parent_ref, quad_ref, fine_ref, down_ref,
    x_ref, pre_ref, act_ref, send_ref, select_s, down_s, act_s,
):
    step = pl.program_id(0)
    base = step * CHUNK
    count = count_ref[0]

    @pl.when(step == 0)
    def _():
        fill_select(select_s)
        spread_weight(down_ref, down_s)
        send_ref[...] = jnp.full(send_ref.shape, -1.0, BF16)

    x_taps = taps_to_lanes(mm_nt(select_s[...], fine_ref[...].reshape(CHUNK * 32, 256)).astype(BF16))
    x_ref[...] = x_taps
    pre = to_rows(mm(x_taps, down_s[...]))
    pre_ref[...] = pre
    act = (pre * sigmoid(pre)).astype(BF16)
    act_ref[...] = act
    act_s[...] = act.astype(F32)
    place = lax.broadcasted_iota(jnp.int32, (8, 128), 0)
    for tile in range(CHUNK):
        parent, quad = parent_ref[base + tile], quad_ref[base + tile]
        owner = parent // coarse_dev
        cell = (parent - owner * coarse_dev) * 4 + quad
        row, col = read_edges(act_s, tile, quad)
        col = jnp.where(place == 7, cell.astype(F32), col)

        @pl.when(base + tile < count)
        def _():
            send_ref[owner] = jnp.concatenate([row, col], axis=0).astype(BF16)


def local_conv(
    count_ref, act_ref, cot_ref, up_ref, mid_ref, g_ref, grad_out_ref, local_ref,
    select_s, up_s, mid_s,
):
    step = pl.program_id(0)

    @pl.when(step == 0)
    def _():
        fill_select(select_s)
        spread_weight(up_ref, up_s)
        for sy in range(3):
            for sx in range(3):
                mid_s[sx * 128 : (sx + 1) * 128, sy * 128 : (sy + 1) * 128] = mid_ref[3 * sy + sx]

    g_taps = mm_nt(select_s[...], cot_ref[...].reshape(CHUNK * 32, 256))
    tile_of = lax.broadcasted_iota(jnp.int32, g_taps.shape, 1) // 32 + step * CHUNK
    g_taps = taps_to_lanes(jnp.where(tile_of < count_ref[0], g_taps, 0.0).astype(BF16))
    g_ref[...] = g_taps
    grad_out_ref[...] = to_rows(mm(g_taps, up_s[...])).astype(BF16)
    parts = mm(side_steps(act_ref[...].astype(F32), False), mid_s[...])
    local_ref[...] = (
        row_step(parts[:, :128], -1) + parts[:, 128:256] + row_step(parts[:, 256:], 1)
    )


def gather_edges(tag_ref, got_ref, edge_s, number):
    def take(slot, carry):
        tag = tag_ref[slot]
        cell = jnp.where(tag < 0, number * 4, tag)
        tile, quad = cell // 4, cell % 4
        block = got_ref[slot].astype(F32)
        at = pl.ds(pl.multiple_of(tile * 8, 8), 8)
        edge_s[0, quad, at, :] = block[:8]
        edge_s[1, quad, at, :] = jnp.where(quad >= 2, pltpu.roll(block[8:], 1, 0), block[8:])
        return carry

    edge_s[...] = jnp.zeros_like(edge_s)
    lax.fori_loop(0, got_ref.shape[0], take, 0, unroll=8)


def scatter_edges(tag_ref, reply_s, send_ref, number):
    def give(slot, carry):
        tag = tag_ref[slot]
        cell = jnp.where(tag < 0, number * 4, tag)
        tile, quad = cell // 4, cell % 4
        at = pl.ds(pl.multiple_of(tile * 8, 8), 8)
        parts = [reply_s[kind, quad, at, :] for kind in range(2)]
        send_ref[slot] = jnp.concatenate(parts, axis=0).astype(BF16)
        return carry

    lax.fori_loop(0, send_ref.shape[0], give, 0, unroll=8)


def corner(x, at):
    return jnp.broadcast_to(x[:, at : at + 1, :], x.shape)


def pack(parts):
    rows = parts[0].shape[0] * 8
    return jnp.concatenate([part.reshape(rows, 128).astype(BF16) for part in parts], axis=1)


def edges_of(edge_s, number):
    rows, cols = [], []
    for quad in range(4):
        at_y, at_x = place_of(quad)
        row = edge_s[0, quad, : number * 8, :].reshape(number, 8, 128)
        col = edge_s[1, quad, : number * 8, :].reshape(number, 8, 128)
        place = lax.broadcasted_iota(jnp.int32, row.shape, 1)
        rows.append(row)
        cols.append(jnp.where(place == at_y, corner(row, at_x), col))
    return rows, cols


def write_reply(reply_s, quad, row, col):
    at_y, at_x = place_of(quad)
    rows = row.shape[0] * 8
    place = lax.broadcasted_iota(jnp.int32, row.shape, 1)
    row = row + jnp.where(place == at_x, corner(col, at_y), 0.0)
    reply_s[0, quad, :rows, :] = row.reshape(rows, 128)
    reply_s[1, quad, :rows, :] = jnp.where(place == at_y, 0.0, col).reshape(rows, 128)


def cross_mid(tag_ref, got_ref, mid_ref, send_ref, act_ref, edge_s, reply_s):
    number = edge_s.shape[2] // 8 - 1
    gather_edges(tag_ref, got_ref, edge_s, number)
    act_row, act_col = edges_of(edge_s, number)
    for quad in range(4):
        low, right = quad // 2, quad % 2
        act_ref[0, quad] = act_row[quad].reshape(number * 8, 128).astype(BF16)
        act_ref[1, quad] = act_col[quad].reshape(number * 8, 128).astype(BF16)
        across, beyond, beside = act_row[quad ^ 2], act_row[quad ^ 3], act_col[quad ^ 1]
        fills = [beyond if right == 1 else None, None, beyond if right == 0 else None]
        sy, sx = 2 - 2 * low, 2 - 2 * right
        patch = pack([shift8(across, s - 1, fills[s]) for s in range(3)])
        weight = jnp.concatenate([mid_ref[3 * sy + s] for s in range(3)], axis=0)
        row = mm(patch, weight).reshape(number, 8, 128)
        patch = pack([shift8(beside, s - 1) for s in range(3)])
        weight = jnp.concatenate([mid_ref[3 * s + sx] for s in range(3)], axis=0)
        col = mm(patch, weight).reshape(number, 8, 128)
        write_reply(reply_s, quad, row, col)
    reply_s[:, :, number * 8 :, :] = jnp.zeros((2, 4, 8, 128), F32)
    scatter_edges(tag_ref, reply_s, send_ref, number)


def cross_grad(tag_ref, got_ref, mid_ref, act_ref, send_ref, cross_ref, edge_s, reply_s):
    number = edge_s.shape[2] // 8 - 1
    gather_edges(tag_ref, got_ref, edge_s, number)
    grad_row, grad_col = edges_of(edge_s, number)
    cross_ref[...] = jnp.zeros_like(cross_ref)
    for quad in range(4):
        low, right = quad // 2, quad % 2
        across, beyond, beside = grad_row[quad ^ 2], grad_row[quad ^ 3], grad_col[quad ^ 1]
        fills = [beyond if right == 0 else None, None, beyond if right == 1 else None]
        sy, sx = 2 * low, 2 * right
        patch = pack([shift8(across, 1 - s, fills[s]) for s in range(3)])
        weight = jnp.concatenate([mid_ref[3 * sy + s] for s in range(3)], axis=1)
        row = mm_nt(patch, weight).reshape(number, 8, 128)
        cross_ref[sy * 128 : (sy + 1) * 128, :] += mm_tn(act_ref[0, quad], patch)
        patch = pack([shift8(beside, 1 - s) for s in range(3)])
        weight = jnp.concatenate([mid_ref[3 * s + sx] for s in range(3)], axis=1)
        col = mm_nt(patch, weight).reshape(number, 8, 128)
        part = mm_tn(act_ref[1, quad], patch)
        for s in range(3):
            cross_ref[s * 128 : (s + 1) * 128, sx * 128 : (sx + 1) * 128] += (
                part[:, s * 128 : (s + 1) * 128]
            )
        write_reply(reply_s, quad, row, col)
    reply_s[:, :, number * 8 :, :] = jnp.zeros((2, 4, 8, 128), F32)
    scatter_edges(tag_ref, reply_s, send_ref, number)


def mid_slopes(
    coarse_dev, count_ref, parent_ref, quad_ref, local_ref, act_ref, grad_out_ref, got_ref,
    out_ref, grad_ref, send_ref, mid_s,
):
    step = pl.program_id(0)
    base = step * CHUNK
    count = count_ref[0]

    @pl.when(step == 0)
    def _():
        send_ref[...] = jnp.zeros(send_ref.shape, BF16)

    mid_s[...] = local_ref[...]
    add_edges(mid_s, got_ref, base, coarse_dev, count, parent_ref, quad_ref)
    mid = mid_s[...]
    gate = sigmoid(mid)
    out_ref[...] = (act_ref[...].astype(F32) + mid * gate).astype(BF16)
    grad = grad_out_ref[...].astype(F32) * (gate * (1.0 + mid * (1.0 - gate)))
    grad = grad.astype(BF16)
    grad_ref[...] = grad
    mid_s[...] = grad.astype(F32)
    for tile in range(CHUNK):
        row, col = read_edges(mid_s, tile, quad_ref[base + tile])

        @pl.when(base + tile < count)
        def _():
            owner = parent_ref[base + tile] // coarse_dev
            send_ref[owner] = jnp.concatenate([row, col], axis=0).astype(BF16)


def local_grads(
    g_ref, out_ref, grad_ref, grad_out_ref, act_ref, mid_ref,
    grad_act_ref, mid_acc, up_ref, up_acc, mid_s,
):
    step = pl.program_id(0)

    @pl.when(step == 0)
    def _():
        mid_acc[...] = jnp.zeros_like(mid_acc)
        up_acc[...] = jnp.zeros_like(up_acc)
        for sy in range(3):
            for sx in range(3):
                mid_s[sy * 128 : (sy + 1) * 128, sx * 128 : (sx + 1) * 128] = mid_ref[3 * sy + sx]

    up_acc[...] += mm_tn(g_ref[...], to_lanes(out_ref[...]))
    steps = side_steps(grad_ref[...].astype(F32), True)
    parts = mm_nt(steps, mid_s[...])
    grad_act_ref[...] = (
        grad_out_ref[...].astype(F32)
        + row_step(parts[:, :128], 1)
        + parts[:, 128:256]
        + row_step(parts[:, 256:], -1)
    )
    act = act_ref[...].astype(F32)
    acts = jnp.concatenate([row_step(act, s - 1).astype(BF16) for s in range(3)], axis=1)
    mid_acc[...] += mm_tn(acts, steps)

    @pl.when(step == pl.num_programs(0) - 1)
    def _():
        fold_taps(up_acc, up_ref)


def fold_taps(acc, out_ref):
    for tap in range(4):
        part = jnp.zeros((32, 128), F32)
        for tile in range(4):
            row = tap * 128 + tile * 32
            part += acc[row : row + 32, tile * 128 : (tile + 1) * 128]
        out_ref[tap * 32 : (tap + 1) * 32, :] = part


def fine_grads(
    coarse_dev, count_ref, parent_ref, quad_ref, cot_ref, x_ref, pre_ref, grad_act_ref, got_ref,
    down_ref, fine_ref, sum_ref, select_s, down_s, act_s, down_acc,
):
    step = pl.program_id(0)
    base = step * CHUNK
    count = count_ref[0]

    @pl.when(step == 0)
    def _():
        fill_select(select_s)
        spread_weight(down_ref, down_s)
        down_acc[...] = jnp.zeros_like(down_acc)

    act_s[...] = grad_act_ref[...]
    add_edges(act_s, got_ref, base, coarse_dev, count, parent_ref, quad_ref)
    grad_act = act_s[...].astype(BF16).astype(F32)
    grad_pre = to_lanes((grad_act * slope(pre_ref[...])).astype(BF16))
    down_acc[...] += mm_tn(x_ref[...], grad_pre)
    back = lanes_to_taps(mm_nt(grad_pre, down_s[...]))
    high = back.astype(BF16)
    rest = (back - high.astype(F32)).astype(BF16)
    select = select_s[...]
    total = mm_tn(high, select) + mm_tn(rest, select)
    total += cot_ref[...].reshape(CHUNK * 32, 256).astype(F32)
    tile_of = lax.broadcasted_iota(jnp.int32, total.shape, 0) // 32 + base
    total = jnp.where(tile_of < count, total, 0.0)
    fine_ref[...] = total.astype(BF16).reshape(CHUNK, 32, 256)

    @pl.when(step == pl.num_programs(0) - 1)
    def _():
        fold_taps(down_acc, sum_ref)


def sum_weights(
    events, plane, depth, pieces, scale, local_ref, cross_ref, up_ref, mid_ref, grad_up_ref,
    mine_ref, near_s, sum_s, far_s, fin_s, low_s, all_s,
    near_send, near_recv, far_send, far_recv, fin_send, fin_recv, all_send, all_recv,
):
    event = lax.axis_index("event")
    tile = lax.axis_index("tile")
    z = tile // plane
    low = tile % plane
    group = events * plane
    me = event * plane + low
    share = mine_ref.shape[0] // group
    piece = share // pieces
    for tap in range(9):
        at = slice(tap // 3 * 128, tap // 3 * 128 + 128), slice(tap % 3 * 128, tap % 3 * 128 + 128)
        mine_ref[tap * 128 : (tap + 1) * 128, :] = (
            (local_ref[at] + cross_ref[at]) * scale
        ).astype(BF16)
    mine_ref[1152:1280, :] = (up_ref[...] * scale).astype(BF16)
    if mine_ref.shape[0] > 1280:
        mine_ref[1280:, :] = jnp.zeros((mine_ref.shape[0] - 1280, 128), BF16)

    def near_id(p):
        return (p // plane, z * plane + p % plane)

    def far_id(p):
        return (event, p * plane + low)

    barrier = pltpu.get_barrier_semaphore()

    def greet_near(k, carry):
        pl.semaphore_signal(
            barrier, inc=1, device_id=near_id((me + k) % group), device_id_type=MESH
        )
        return carry

    def greet_far(k, carry):
        pl.semaphore_signal(
            barrier, inc=1, device_id=far_id((z + k) % depth), device_id_type=MESH
        )
        return carry

    lax.fori_loop(1, group, greet_near, 0)
    lax.fori_loop(1, depth, greet_far, 0)
    pl.semaphore_wait(barrier, group + depth - 2)

    def rows(p):
        return pl.ds(pl.multiple_of(p * share, 16), share)

    def near_copy(to, slot):
        return pltpu.make_async_remote_copy(
            src_ref=mine_ref.at[rows(to)],
            dst_ref=near_s.at[slot],
            send_sem=near_send.at[to],
            recv_sem=near_recv.at[slot],
            device_id=near_id(to),
            device_id_type=MESH,
        )

    def send_near(k, carry):
        near_copy((me + k) % group, me).start()
        return carry

    lax.fori_loop(1, group, send_near, 0)

    def take_near(k, total):
        p = (me + k) % group
        near_copy(p, p).wait_recv()
        return total + near_s[p].astype(F32)

    total = lax.fori_loop(1, group, take_near, mine_ref[rows(me), :].astype(F32))
    sum_s[...] = total.reshape(pieces, piece, 128)

    def far_copy(to, slot):
        return pltpu.make_async_remote_copy(
            src_ref=sum_s.at[to],
            dst_ref=far_s.at[slot],
            send_sem=far_send.at[to],
            recv_sem=far_recv.at[slot],
            device_id=far_id(to),
            device_id_type=MESH,
        )

    for to in range(pieces):

        @pl.when(z != to)
        def _():
            far_copy(to, z).start()

    def fin_copy(to, slot):
        return pltpu.make_async_remote_copy(
            src_ref=fin_s.at[slot],
            dst_ref=fin_s.at[slot],
            send_sem=fin_send.at[to],
            recv_sem=fin_recv.at[slot],
            device_id=far_id(to),
            device_id_type=MESH,
        )

    @pl.when(z < pieces)
    def _():
        def take_far(k, total):
            p = (z + k) % depth
            far_copy(z, p).wait_recv()
            return total + far_s[p]

        fin_s[z] = lax.fori_loop(1, depth, take_far, sum_s[z])

        def send_fin(k, carry):
            fin_copy((z + k) % depth, z).start()
            return carry

        lax.fori_loop(1, depth, send_fin, 0)

    for p in range(pieces):

        @pl.when(z != p)
        def _():
            fin_copy(p, p).wait_recv()

    low_s[...] = fin_s[...].reshape(share, 128).astype(BF16)

    def all_copy(to, slot):
        return pltpu.make_async_remote_copy(
            src_ref=low_s,
            dst_ref=all_s.at[rows(slot)],
            send_sem=all_send.at[to],
            recv_sem=all_recv.at[slot],
            device_id=near_id(to),
            device_id_type=MESH,
        )

    def send_all(k, carry):
        all_copy((me + k) % group, me).start()
        return carry

    lax.fori_loop(1, group, send_all, 0)
    all_s[rows(me), :] = low_s[...]

    def take_all(k, carry):
        p = (me + k) % group
        all_copy(p, p).wait_recv()
        return carry

    lax.fori_loop(1, group, take_all, 0)
    mid_ref[...] = all_s[:1152, :].astype(F32)
    grad_up_ref[...] = all_s[1152:1280, :].astype(F32)

    def sent_near(k, carry):
        p = (me + k) % group
        near_copy(p, me).wait_send()
        all_copy(p, me).wait_send()
        return carry

    lax.fori_loop(1, group, sent_near, 0)
    for to in range(pieces):

        @pl.when(z != to)
        def _():
            far_copy(to, z).wait_send()

    @pl.when(z < pieces)
    def _():
        def sent_fin(k, carry):
            fin_copy((z + k) % depth, z).wait_send()
            return carry

        lax.fori_loop(1, depth, sent_fin, 0)


def sum_down(
    events, plane, depth, scale, mine_ref, total_ref, mine_s, near_s, low_s, far_s, fin_s, all_s,
    near_send, near_recv, far_send, far_recv, all_send, all_recv,
):
    event = lax.axis_index("event")
    tile = lax.axis_index("tile")
    z = tile // plane
    group = events * plane
    me = event * plane + tile % plane
    pieces = mine_ref.shape[0] // 16
    stride = group // pieces
    my_piece = me // stride
    reducer = me % stride == 0

    def near_id(p):
        return (p // plane, z * plane + p % plane)

    def far_id(p):
        return (event, p * plane + tile % plane)

    barrier = pltpu.get_barrier_semaphore()

    def greet(to):
        pl.semaphore_signal(barrier, inc=1, device_id=to, device_id_type=MESH)

    @pl.when(reducer)
    def _():
        def near(k, carry):
            greet(near_id((me + k) % group))
            return carry

        def far(k, carry):
            greet(far_id((z + k) % depth))
            return carry

        lax.fori_loop(1, group, near, 0)
        lax.fori_loop(1, depth, far, 0)

    @pl.when(me % stride != 0)
    def _():
        for p in range(pieces):
            greet(near_id(p * stride))

    mine_s[...] = (mine_ref[...] * scale).astype(BF16).reshape(mine_s.shape)

    @pl.when(reducer)
    def _():
        pl.semaphore_wait(barrier, group + depth - 2)

    @pl.when(me % stride != 0)
    def _():
        pl.semaphore_wait(barrier, pieces)

    def near_copy(piece, slot):
        return pltpu.make_async_remote_copy(
            src_ref=mine_s.at[piece],
            dst_ref=near_s.at[slot],
            send_sem=near_send.at[piece],
            recv_sem=near_recv.at[slot],
            device_id=near_id(piece * stride),
            device_id_type=MESH,
        )

    def far_copy(to, slot):
        return pltpu.make_async_remote_copy(
            src_ref=low_s,
            dst_ref=far_s.at[slot],
            send_sem=far_send.at[to],
            recv_sem=far_recv.at[slot],
            device_id=far_id(to),
            device_id_type=MESH,
        )

    def all_copy(to, piece):
        return pltpu.make_async_remote_copy(
            src_ref=fin_s,
            dst_ref=all_s.at[piece],
            send_sem=all_send.at[to],
            recv_sem=all_recv.at[piece],
            device_id=near_id(to),
            device_id_type=MESH,
        )

    for piece in range(pieces):

        @pl.when(me != piece * stride)
        def _():
            near_copy(piece, me).start()

    @pl.when(reducer)
    def _():
        def take_near(k, total):
            p = (me + k) % group
            near_copy(my_piece, p).wait_recv()
            return total + near_s[p].astype(F32)

        total = lax.fori_loop(1, group, take_near, mine_s[my_piece].astype(F32))
        low_s[...] = total.astype(BF16)

        def send_far(k, carry):
            far_copy((z + k) % depth, z).start()
            return carry

        lax.fori_loop(1, depth, send_far, 0)
        far_s[z] = low_s[...]

        def take_far(k, carry):
            p = (z + k) % depth
            far_copy(p, p).wait_recv()
            return carry

        lax.fori_loop(1, depth, take_far, 0)
        final = jnp.sum(far_s[...].astype(F32), axis=0)
        fin_s[...] = final.astype(BF16)

        def send_all(k, carry):
            all_copy((me + k) % group, my_piece).start()
            return carry

        lax.fori_loop(1, group, send_all, 0)
        all_s[my_piece] = fin_s[...]

    for piece in range(pieces):

        @pl.when(me != piece * stride)
        def _():
            all_copy(me, piece).wait_recv()

    total_ref[...] = all_s[...].reshape(total_ref.shape).astype(F32)
    for piece in range(pieces):

        @pl.when(me != piece * stride)
        def _():
            near_copy(piece, me).wait_send()

    @pl.when(reducer)
    def _():
        def sent_far(k, carry):
            far_copy((z + k) % depth, z).wait_send()
            return carry

        def sent_all(k, carry):
            all_copy((me + k) % group, my_piece).wait_send()
            return carry

        lax.fori_loop(1, depth, sent_far, 0)
        lax.fori_loop(1, group, sent_all, 0)


def full(shape):
    return pl.BlockSpec(shape, lambda *_: (0,) * len(shape))


def chunked(shape):
    return pl.BlockSpec(shape, lambda step, *_: (step,) + (0,) * (len(shape) - 1))


def like(shape, dtype):
    return jax.ShapeDtypeStruct(shape, dtype)


def gridded(body, name, steps, scalars, arrays, in_specs, outs, scratch, flops, limit=VMEM_LIMIT):
    return pl.pallas_call(
        body,
        grid_spec=pltpu.PrefetchScalarGridSpec(
            num_scalar_prefetch=len(scalars),
            grid=(steps,),
            in_specs=in_specs,
            out_specs=[spec for spec, _ in outs],
            scratch_shapes=scratch,
        ),
        out_shape=[shape for _, shape in outs],
        compiler_params=pltpu.CompilerParams(vmem_limit_bytes=limit),
        cost_estimate=pl.CostEstimate(
            flops=flops, bytes_accessed=8 * 1024 * 1024, transcendentals=0
        ),
        name=name,
    )(*scalars, *arrays)


def whole(body, name, arrays, in_specs, outs, scratch, collective=None):
    params = dict(vmem_limit_bytes=VMEM_LIMIT)
    if collective is not None:
        params.update(collective_id=collective, has_side_effects=True)
    vmem = pl.BlockSpec(memory_space=pltpu.VMEM)
    return pl.pallas_call(
        body,
        in_specs=in_specs,
        out_specs=[vmem] * len(outs),
        out_shape=outs,
        scratch_shapes=scratch,
        compiler_params=pltpu.CompilerParams(**params),
        cost_estimate=pl.CostEstimate(
            flops=4 * 10**9, bytes_accessed=4 * 1024 * 1024, transcendentals=0
        ),
        name=name,
    )(*arrays)


def exchange(x):
    return lax.all_to_all(x, "tile", split_axis=0, concat_axis=0, tiled=True)


def shards(plane, fine, cotangent, counts, parent, quadrant, down_weight, mid_weight, up_weight):
    number = fine.shape[1]
    slots = lax.axis_size("tile")
    events = lax.axis_size("event")
    coarse_dev = number // 4
    rows = number * PIXELS
    steps = number // CHUNK
    step_rows = CHUNK * PIXELS
    scale = 1.0 / math.sqrt(events * slots * number * 64)
    scalars = (counts[0], parent[0], quadrant[0])
    message = like((slots, EDGE_ROWS, 128), BF16)
    messages = full((slots, EDGE_ROWS, 128))
    tiles = chunked((CHUNK, 32, 256))
    taps = chunked((step_rows // 4, 512))
    pixels = chunked((step_rows, 128))
    taps_shape = like((rows // 4, 512), BF16)
    wide, narrow = like((rows, 128), F32), like((rows, 128), BF16)
    thin, square = full((4, 32, 128)), full((9, 128, 128))
    smem = pl.BlockSpec(memory_space=pltpu.SMEM)
    vmem = pl.BlockSpec(memory_space=pltpu.VMEM)
    spread = pltpu.VMEM((512, 512), BF16)
    nine = pltpu.VMEM((384, 384), BF16)
    pixel_s = pltpu.VMEM((step_rows, 128), F32)
    select_s = pltpu.VMEM((256, 256), BF16)
    edge_s = pltpu.VMEM((2, 4, coarse_dev * 8 + 8, 128), F32)
    edges = like((2, 4, coarse_dev * 8, 128), BF16)

    x_taps, pre, act, act_edges = gridded(
        functools.partial(down_conv, coarse_dev),
        "down_conv",
        steps,
        scalars,
        (fine[0], down_weight),
        [tiles, thin],
        [(taps, taps_shape), (pixels, wide), (pixels, narrow), (messages, message)],
        [select_s, spread, pixel_s],
        10**9,
        FIRST_LIMIT,
    )
    got = exchange(act_edges)
    g_taps, grad_out, local = gridded(
        local_conv,
        "local_conv",
        steps,
        scalars[:1],
        (act, cotangent[0], up_weight, mid_weight),
        [pixels, tiles, thin, square],
        [(taps, taps_shape), (pixels, narrow), (pixels, wide)],
        [select_s, spread, nine],
        4 * 10**9,
    )
    tags = got[:, EDGE_ROWS - 1, 0].astype(jnp.int32)
    reply, act_edges = whole(
        cross_mid, "cross_mid", (tags, got, mid_weight), [smem, vmem, vmem],
        [message, edges], [edge_s, edge_s],
    )
    got = exchange(reply)
    out, grad, grad_edges = gridded(
        functools.partial(mid_slopes, coarse_dev),
        "mid_slopes",
        steps,
        scalars,
        (local, act, grad_out, got),
        [pixels, pixels, pixels, messages],
        [(pixels, narrow), (pixels, narrow), (messages, message)],
        [pixel_s],
        10**9,
    )
    got = exchange(grad_edges)
    grad_act, grad_mid, grad_up = gridded(
        local_grads,
        "local_grads",
        steps,
        (),
        (g_taps, out, grad, grad_out, act, mid_weight),
        [taps, pixels, pixels, pixels, pixels, square],
        [
            (pixels, wide),
            (full((384, 384)), like((384, 384), F32)),
            (full((128, 128)), like((128, 128), F32)),
        ],
        [pltpu.VMEM((512, 512), F32), nine],
        6 * 10**9,
    )
    reply, cross = whole(
        cross_grad, "cross_grad", (tags, got, mid_weight, act_edges), [smem, vmem, vmem, vmem],
        [message, like((384, 384), F32)], [edge_s, edge_s],
    )
    got = exchange(reply)

    group = events * plane
    depth = slots // plane
    share = -(-1280 // (group * 16)) * 16
    pieces = max(n for n in range(1, share // 8 + 1) if share // 8 % n == 0 and n <= depth)
    piece = share // pieces
    dma = pltpu.SemaphoreType.DMA
    grad_mid, grad_up = whole(
        functools.partial(sum_weights, events, plane, depth, pieces, scale),
        "sum_weights",
        (grad_mid, cross, grad_up),
        [vmem] * 3,
        [like((1152, 128), F32), like((128, 128), F32)],
        [
            pltpu.VMEM((group * share, 128), BF16),
            pltpu.VMEM((group, share, 128), BF16),
            pltpu.VMEM((pieces, piece, 128), F32),
            pltpu.VMEM((depth, piece, 128), F32),
            pltpu.VMEM((pieces, piece, 128), F32),
            pltpu.VMEM((share, 128), BF16),
            pltpu.VMEM((group * share, 128), BF16),
            dma((group,)),
            dma((group,)),
            dma((pieces,)),
            dma((depth,)),
            dma((depth,)),
            dma((pieces,)),
            dma((group,)),
            dma((group,)),
        ],
        0,
    )
    grad_fine, grad_down = gridded(
        functools.partial(fine_grads, coarse_dev),
        "fine_grads",
        steps,
        scalars,
        (cotangent[0], x_taps, pre, grad_act, got, down_weight),
        [tiles, taps, pixels, pixels, messages, thin],
        [(tiles, like((number, 32, 256), BF16)), (full((128, 128)), like((128, 128), F32))],
        [select_s, spread, pixel_s, pltpu.VMEM((512, 512), F32)],
        4 * 10**9,
    )
    (grad_down,) = whole(
        functools.partial(sum_down, events, plane, depth, scale),
        "sum_down",
        (grad_down,),
        [vmem],
        [like((128, 128), F32)],
        [
            pltpu.VMEM((8, 16, 128), BF16),
            pltpu.VMEM((group, 16, 128), BF16),
            pltpu.VMEM((16, 128), BF16),
            pltpu.VMEM((depth, 16, 128), BF16),
            pltpu.VMEM((16, 128), BF16),
            pltpu.VMEM((8, 16, 128), BF16),
            dma((8,)),
            dma((group,)),
            dma((depth,)),
            dma((depth,)),
            dma((group,)),
            dma((8,)),
        ],
        1,
    )
    return (
        grad_fine[None],
        grad_down.reshape(4, 32, 128),
        grad_mid.reshape(9, 128, 128),
        grad_up.reshape(4, 32, 128),
    )


def solution(mesh):
    placed = (
        P("event", "tile", None, None),
        P("event", "tile", None, None),
        P("event", "tile"),
        P("event", "tile"),
        P("event", "tile"),
        P(),
        P(),
        P(),
    )
    return jax.shard_map(
        functools.partial(shards, 8),
        mesh=mesh,
        in_specs=placed,
        out_specs=(P("event", "tile", None, None), P(), P(), P()),
        check_vma=False,
    )
```

time: 257 us -> 268 us (1.043)
  waiting for transfers between devices: 73.5 us -> 22 us
  Pallas kernels: 85.9 us -> 117 us
  blocking collectives: 62.7 us -> 90.8 us
  local copies, waits for them, and re-layouts: 9.14 us -> 15 us
    all_to_all x1 -> x2, waiting for transfers between devices: 73.5 us -> 22 us  [exchange(): return lax.all_to_all(x, 'tile', split_axis=0, concat_axis=0, tiled=True)]
    pallas_call x4 -> x9, Pallas kernels: 85.9 us -> 117 us  [the longest x4 77 us: whole(): pl.pallas_call(body, in_specs=in_specs, out_specs=[vmem] * len(outs), out...]
    all_to_all x1 -> x2, blocking collectives: 62.7 us -> 90.8 us  [exchange(): return lax.all_to_all(x, 'tile', split_axis=0, concat_axis=0, tiled=True)]
    unnamed x30 -> x45, local copies, waits for them, and re-layouts: 7.41 us -> 15 us
    all_to_all x1 -> x2, starting transfers between devices: 20.7 us -> 18.2 us  [exchange(): return lax.all_to_all(x, 'tile', split_axis=0, concat_axis=0, tiled=True)]
  transfers between devices with their start and end apart: 1 -> 2, of which waited for: 1 -> 1; matrix products, arithmetic and copies ran while one was open for 0% -> 0% of each run, Pallas kernels for 0% -> 21%
where the time goes in v2:
time: 268 us; the launch traced here: 267 us
  Pallas kernels  117 us (44%)
  blocking collectives  90.8 us (34%)
  waiting for transfers between devices  22 us (8%)
  starting transfers between devices  18.2 us (7%)
  local copies, waits for them, and re-layouts  15 us (6%)
    all_to_all x2, blocking collectives, exchange(): return lax.all_to_all(x, 'tile', split_axis=0, concat_axis=0, tiled=True)  90.8 us
    pallas_call x4, Pallas kernels, whole(): pl.pallas_call(body, in_specs=in_specs, out_specs=[vmem] * len(outs), out...  77 us
    pallas_call x5, Pallas kernels, gridded(): pl.pallas_call(body, grid_spec=pltpu.PrefetchScalarGridSpec(num_scalar_pr...  39.7 us
    all_to_all x2, waiting for transfers between devices, exchange(): return lax.all_to_all(x, 'tile', split_axis=0, concat_axis=0, tiled=True)  22 us
    all_to_all x2, starting transfers between devices, exchange(): return lax.all_to_all(x, 'tile', split_axis=0, concat_axis=0, tiled=True)  18.2 us
    unnamed x45, local copies, waits for them, and re-layouts  15 us
  transfers between devices with their start and end apart: 2, of which 1 were waited for; matrix products, arithmetic and copies ran while one was open for 0% of the time, Pallas kernels for 21%

profile of v2, /device:TPU:1, one launch (start us, length us, event | category | flops | bytes accessed | tf_op | source)
XLA Modules:
  0.0 266.6 jit_solution(5457655438625218942)
XLA Ops:
  1.3 0.0 copy-start.10
  1.3 8.2 %down_conv.1 = (bf16[1280,512]{1,0:T(8,128)(2,1)}, f32[5120,128]{1,0:T(8,128)}, bf16[5120,128]{1,0:T(8,128)(2,1)}, bf16[128,16,128]{2,1,0:T(8,128)(2,1)}) custom-call(s32[1]{0:T(128)} %bitcast.9.count_ref, s32[80]{0:T(128)} %bitcast.16, s32[80]{0:T(128)} %bitcast.19, bf16[80,32,256]{2,1,0:T(8,128)(2,1)} %bitcast.24, bf16[4,32,128]{2,1,0:T(8,128)(2,1)} %down_ref.3), custom_call_target="tpu_custom_call" | custom-call | flops 1000000000 | bytes 8388608 | tf_op jit(solution)/shard_map/down_conv/pallas_call | solution.py:759
  9.5 51.4 %all_to_all.20.got_ref = bf16[128,16,128]{2,1,0:T(8,128)(2,1)S(1)} all-to-all(bf16[128,16,128]{2,1,0:T(8,128)(2,1)} %get-tuple-element.31), channel_id=1, replica_groups=mesh['event'=4,'tile'=128] {'tile'}, dimensions={0} | all-to-all | bytes 1048576 | tf_op jit(solution)/shard_map/all_to_all | solution.py:797
  60.9 2.4 fusion.tag_ref
  63.3 0.0 copy-done.10
  63.3 0.0 copy-start
  63.3 0.0 copy-start.5
  63.3 0.0 copy-start.11
  63.3 3.9 %cross_mid.1 = (bf16[128,16,128]{2,1,0:T(8,128)(2,1)}, bf16[2,4,160,128]{3,2,1,0:T(8,128)(2,1)S(1)}) custom-call(s32[128]{0:T(128)S(1)} %fusion.tag_ref, bf16[128,16,128]{2,1,0:T(8,128)(2,1)S(1)} %all_to_all.20.got_ref, bf16[9,128,128]{2,1,0:T(8,128)(2,1)S(1)} %copy-done.10), custom_call_target="tpu_custom_call" | custom-call | flops 4000000000 | bytes 4194304 | tf_op jit(solution)/shard_map/cross_mid/pallas_call | solution.py:782
  67.2 0.7 copy-done.19
  67.9 9.1 %all-to-all-start.1 = ((bf16[128,16,128]{2,1,0:T(8,128)(2,1)}), bf16[128,16,128]{2,1,0:T(8,128)(2,1)S(1)}, u32[]{:S(2)}, u32[]{:S(2)}) async-start(bf16[128,16,128]{2,1,0:T(8,128)(2,1)} %get-tuple-element.32), calls=%async_computation.1 | async-start | bytes 1048576 | tf_op jit(solution)/shard_map/all_to_all | solution.py:797
  77.0 0.0 copy-done
  77.0 0.0 copy-done.5
  77.0 0.0 copy-done.11
  77.0 0.0 copy-start.3
  77.1 0.0 copy-start.4
  77.1 6.5 %local_conv.1 = (bf16[1280,512]{1,0:T(8,128)(2,1)S(1)}, bf16[5120,128]{1,0:T(8,128)(2,1)S(1)}, f32[5120,128]{1,0:T(8,128)}) custom-call(s32[1]{0:T(128)} %bitcast.10.count_ref, bf16[5120,128]{1,0:T(8,128)(2,1)S(1)} %copy-done, bf16[80,32,256]{2,1,0:T(8,128)(2,1)S(1)} %bitcast.22, bf16[4,32,128]{2,1,0:T(8,128)(2,1)S(1)} %copy-done.11, ...), custom_call_target="tpu_custom_call" | custom-call | flops 4000000000 | bytes 8388608 | tf_op jit(solution)/shard_map/local_conv/pallas_call | solution.py:759
  83.6 1.2 copy-done.1
  84.7 1.1 copy-done.15
  85.8 22.0 %all-to-all-done.1.got_ref = bf16[128,16,128]{2,1,0:T(8,128)(2,1)S(1)} async-done(((bf16[128,16,128]{2,1,0:T(8,128)(2,1)}), bf16[128,16,128]{2,1,0:T(8,128)(2,1)S(1)}, u32[]{:S(2)}, u32[]{:S(2)}) %all-to-all-start.1) | async-done | bytes 524320 | tf_op jit(solution)/shard_map/all_to_all | solution.py:797
  107.8 0.0 copy-done.3
  107.8 0.0 copy-done.4
  107.8 7.7 %mid_slopes.1 = (bf16[5120,128]{1,0:T(8,128)(2,1)S(1)}, bf16[5120,128]{1,0:T(8,128)(2,1)S(1)}, bf16[128,16,128]{2,1,0:T(8,128)(2,1)S(1)}) custom-call(s32[1]{0:T(128)} %bitcast.11.count_ref, s32[80]{0:T(128)S(1)} %bitcast.17, s32[80]{0:T(128)S(1)} %bitcast.20, f32[5120,128]{1,0:T(8,128)} %get-tuple-element.29.local_ref, bf16[5120,128]{1,0:T(8,128)(2,1)S(1)} %copy-done, ...), custom_call_target="tpu_custom_call" | custom-call | flops 1000000000 | bytes 8388608 | tf_op jit(solution)/shard_map/mid_slopes/pallas_call | solution.py:759
  115.6 0.0 copy-start.6
  115.6 1.1 copy-done.6
  116.6 1.1 copy-done.8
  117.7 39.4 %all_to_all.21.got_ref = bf16[128,16,128]{2,1,0:T(8,128)(2,1)S(1)} all-to-all(bf16[128,16,128]{2,1,0:T(8,128)(2,1)S(1)} %get-tuple-element.36), channel_id=1, replica_groups=mesh['event'=4,'tile'=128] {'tile'}, dimensions={0} | all-to-all | bytes 1048576 | tf_op jit(solution)/shard_map/all_to_all | solution.py:797
  157.1 0.0 copy-done.20
  157.1 4.2 %cross_grad.1 = (bf16[128,16,128]{2,1,0:T(8,128)(2,1)}, f32[384,384]{1,0:T(8,128)S(1)}) custom-call(s32[128]{0:T(128)S(1)} %fusion.tag_ref, bf16[128,16,128]{2,1,0:T(8,128)(2,1)S(1)} %all_to_all.21.got_ref, bf16[9,128,128]{2,1,0:T(8,128)(2,1)S(1)} %copy-done.10, bf16[2,4,160,128]{3,2,1,0:T(8,128)(2,1)S(1)} %copy-done.20), custom_call_target="tpu_custom_call" | custom-call | flops 4000000000 | bytes 4194304 | tf_op jit(solution)/shard_map/cross_grad/pallas_call | solution.py:782
  161.3 0.8 copy-done.17
  162.1 9.1 %all-to-all-start.3 = ((bf16[128,16,128]{2,1,0:T(8,128)(2,1)}), bf16[128,16,128]{2,1,0:T(8,128)(2,1)S(1)}, u32[]{:S(2)}, u32[]{:S(2)}) async-start(bf16[128,16,128]{2,1,0:T(8,128)(2,1)} %get-tuple-element.38), calls=%async_computation.3 | async-start | bytes 1048576 | tf_op jit(solution)/shard_map/all_to_all | solution.py:797
  171.2 0.0 copy-done.2
  171.2 0.0 copy-start.7
  171.2 1.3 copy-done.7
  172.6 1.3 copy-done.9
  173.9 1.3 copy-done.16
  175.2 8.2 %local_grads.1 = (f32[5120,128]{1,0:T(8,128)}, f32[384,384]{1,0:T(8,128)S(1)}, f32[128,128]{1,0:T(8,128)S(1)}) custom-call(bf16[1280,512]{1,0:T(8,128)(2,1)S(1)} %copy-done.16, bf16[5120,128]{1,0:T(8,128)(2,1)S(1)} %copy-done.7, bf16[5120,128]{1,0:T(8,128)(2,1)S(1)} %copy-done.9, bf16[5120,128]{1,0:T(8,128)(2,1)S(1)} %copy-done.2, ...), custom_call_target="tpu_custom_call" | custom-call | flops 6000000000 | bytes 8388608 | tf_op jit(solution)/shard_map/local_grads/pallas_call | solution.py:759
  183.4 0.0 copy-done.18
  183.4 42.5 %sum_weights.1 = (f32[1152,128]{1,0:T(8,128)S(1)}, f32[128,128]{1,0:T(8,128)S(1)}) custom-call(f32[384,384]{1,0:T(8,128)S(1)} %get-tuple-element.41.local_ref, f32[384,384]{1,0:T(8,128)S(1)} %copy-done.18, f32[128,128]{1,0:T(8,128)S(1)} %get-tuple-element.43.up_ref), custom_call_target="tpu_custom_call" | custom-call | flops 4000000000 | bytes 4194304 | tf_op jit(solution)/shard_map/sum_weights/pallas_call | solution.py:782
  225.9 0.0 all-to-all-done.3.got_ref
  225.9 0.0 copy-done.12
  226.0 1.7 copy-done.13
  227.7 1.3 copy-done.14
  229.0 9.1 %fine_grads.1 = (bf16[80,32,256]{2,1,0:T(8,128)(2,1)}, f32[128,128]{1,0:T(8,128)S(1)}) custom-call(s32[1]{0:T(128)} %bitcast.12.count_ref, s32[80]{0:T(128)S(1)} %bitcast.18, s32[80]{0:T(128)S(1)} %bitcast.21, bf16[80,32,256]{2,1,0:T(8,128)(2,1)S(1)} %bitcast.23, bf16[1280,512]{1,0:T(8,128)(2,1)S(1)} %copy-done.14, f32[5120,128]{1,0:T(8,128)S(1)} %copy-done.13, ...), custom_call_target="tpu_custom_call" | custom-call | flops 4000000000 | bytes 8388608 | tf_op jit(solution)/shard_map/fine_grads/pallas_call | solution.py:759
  238.1 26.4 %sum_down.1 = f32[128,128]{1,0:T(8,128)S(1)} custom-call(f32[128,128]{1,0:T(8,128)S(1)} %get-tuple-element.40.mine_ref), custom_call_target="tpu_custom_call" | custom-call | flops 4000000000 | bytes 4194304 | tf_op jit(solution)/shard_map/sum_down/pallas_call | solution.py:782
  264.5 0.6 copy.16
  265.2 0.8 copy.17
  266.0 0.6 copy.18
  (13 shorter events, 0.0 us)
Async XLA Ops:
  1.3 62.0 %copy-start.10 = (bf16[9,128,128]{2,1,0:T(8,128)(2,1)S(1)}, bf16[9,128,128]{2,1,0:T(8,128)(2,1)}, u32[]{:S(2)}) copy-start(bf16[9,128,128]{2,1,0:T(8,128)(2,1)} %mid_ref.7) | copy-start | bytes 884740
  63.3 13.7 %copy-start = (bf16[5120,128]{1,0:T(8,128)(2,1)S(1)}, bf16[5120,128]{1,0:T(8,128)(2,1)}, u32[]{:S(2)}) copy-start(bf16[5120,128]{1,0:T(8,128)(2,1)} %get-tuple-element.27.act_ref) | copy-start | bytes 3932164
  63.3 13.7 %copy-start.5 = (bf16[1,80,32,256]{3,2,1,0:T(8,128)(2,1)S(1)}, bf16[1,80,32,256]{3,2,1,0:T(8,128)(2,1)}, u32[]{:S(2)}) copy-start(bf16[1,80,32,256]{3,2,1,0:T(8,128)(2,1)} %param.9) | copy-start | bytes 3932164
  63.3 13.7 %copy-start.11 = (bf16[4,32,128]{2,1,0:T(8,128)(2,1)S(1)}, bf16[4,32,128]{2,1,0:T(8,128)(2,1)}, u32[]{:S(2)}) copy-start(bf16[4,32,128]{2,1,0:T(8,128)(2,1)} %up_ref.1) | copy-start | bytes 98308
  67.2 0.7 copy-start.19
  67.9 39.9 %all-to-all-start.1 = ((bf16[128,16,128]{2,1,0:T(8,128)(2,1)}), bf16[128,16,128]{2,1,0:T(8,128)(2,1)S(1)}, u32[]{:S(2)}, u32[]{:S(2)}) async-start(bf16[128,16,128]{2,1,0:T(8,128)(2,1)} %get-tuple-element.32), calls=%async_computation.1 | async-start | bytes 1048576 | tf_op jit(solution)/shard_map/all_to_all | solution.py:797
  77.0 30.8 %copy-start.3 = (s32[1,80]{1,0:T(1,128)S(1)}, s32[1,80]{1,0:T(1,128)}, u32[]{:S(2)}) copy-start(s32[1,80]{1,0:T(1,128)} %param.11) | copy-start | bytes 964
  77.1 30.8 %copy-start.4 = (s32[1,80]{1,0:T(1,128)S(1)}, s32[1,80]{1,0:T(1,128)}, u32[]{:S(2)}) copy-start(s32[1,80]{1,0:T(1,128)} %param.12) | copy-start | bytes 964
  83.6 1.2 copy-start.1
  84.7 1.1 copy-start.15
  107.8 49.3 %copy-start.20 = (bf16[2,4,160,128]{3,2,1,0:T(8,128)(2,1)S(1)}, bf16[2,4,160,128]{3,2,1,0:T(8,128)(2,1)}, u32[]{:S(2)}) copy-start(bf16[2,4,160,128]{3,2,1,0:T(8,128)(2,1)} %copy-done.19) | copy-start | bytes 983044
  115.6 1.1 copy-start.6
  116.6 1.1 copy-start.8
  157.1 14.1 %copy-start.2 = (bf16[5120,128]{1,0:T(8,128)(2,1)S(1)}, bf16[5120,128]{1,0:T(8,128)(2,1)}, u32[]{:S(2)}) copy-start(bf16[5120,128]{1,0:T(8,128)(2,1)} %copy-done.1) | copy-start | bytes 3932164
  161.3 0.8 copy-start.17
  162.1 63.8 %all-to-all-start.3 = ((bf16[128,16,128]{2,1,0:T(8,128)(2,1)}), bf16[128,16,128]{2,1,0:T(8,128)(2,1)S(1)}, u32[]{:S(2)}, u32[]{:S(2)}) async-start(bf16[128,16,128]{2,1,0:T(8,128)(2,1)} %get-tuple-element.38), calls=%async_computation.3 | async-start | bytes 1048576 | tf_op jit(solution)/shard_map/all_to_all | solution.py:797
  171.2 1.3 copy-start.7
  172.6 1.3 copy-start.9
  173.9 1.3 copy-start.16
  175.2 8.2 %copy-start.18 = (f32[384,384]{1,0:T(8,128)S(1)}, f32[384,384]{1,0:T(8,128)}, u32[]{:S(2)}) copy-start(f32[384,384]{1,0:T(8,128)} %copy-done.17) | copy-start | bytes 1769476
  183.4 42.6 %copy-start.12 = (bf16[4,32,128]{2,1,0:T(8,128)(2,1)S(1)}, bf16[4,32,128]{2,1,0:T(8,128)(2,1)}, u32[]{:S(2)}) copy-start(bf16[4,32,128]{2,1,0:T(8,128)(2,1)} %down_ref.3) | copy-start | bytes 98308
  226.0 1.7 copy-start.13
  227.7 1.3 copy-start.14

commit v3 on v0

v3 whole, which is shorter than its diff:
```python
import functools
import math

import jax
import jax.numpy as jnp
from jax import lax
from jax.experimental import pallas as pl
from jax.experimental.pallas import tpu as pltpu
from jax.sharding import PartitionSpec as P

MESH = pl.DeviceIdType.MESH
F32 = jnp.float32
BF16 = jnp.bfloat16
CHUNK = 16
PIXELS = 64
EDGE_ROWS = 16
VMEM_LIMIT = 60 * 1024 * 1024


def mm(a, b):
    return jnp.dot(a, b, preferred_element_type=F32)


def mm_nt(a, b):
    return lax.dot_general(a, b, (((1,), (1,)), ((), ())), preferred_element_type=F32)


def mm_tn(a, b):
    return lax.dot_general(a, b, (((0,), (0,)), ((), ())), preferred_element_type=F32)


def sigmoid(v):
    return 0.5 * jnp.tanh(0.5 * v) + 0.5


def slope(v):
    g = sigmoid(v)
    return g * (1.0 + v * (1.0 - g))


def shift8(x, step, fill=None):
    if step == 0:
        return x
    place = lax.broadcasted_iota(jnp.int32, x.shape, 1)
    moved = pltpu.roll(x, 7 if step > 0 else 1, 1)
    outside = place == (7 if step > 0 else 0)
    if fill is None:
        return jnp.where(outside, 0.0, moved)
    return jnp.where(outside, pltpu.roll(fill, 7 if step > 0 else 1, 1), moved)


def side_steps(x, flip):
    blocks = x.reshape(x.shape[0] // 8, 8, 128)
    parts = [shift8(blocks, 1 - s if flip else s - 1) for s in range(3)]
    return jnp.concatenate([part.reshape(x.shape).astype(BF16) for part in parts], axis=1)


def row_step(x, step):
    if step == 0:
        return x
    blocks = x.reshape(x.shape[0] // PIXELS, 8, 8, 128)
    zero = jnp.zeros((blocks.shape[0], 1, 8, 128), x.dtype)
    if step > 0:
        moved = jnp.concatenate([blocks[:, 1:], zero], axis=1)
    else:
        moved = jnp.concatenate([zero, blocks[:, :7]], axis=1)
    return moved.reshape(x.shape)


def spread_weight(weight_ref, spread_ref):
    spread_ref[...] = jnp.zeros_like(spread_ref)
    for tap in range(4):
        for tile in range(4):
            row = tap * 128 + tile * 32
            spread_ref[row : row + 32, tile * 128 : (tile + 1) * 128] = weight_ref[tap]


def to_lanes(x):
    groups = x.shape[0] // (4 * PIXELS)
    rows = []
    for group in range(groups):
        parts = [
            x[(group * 4 + tile) * PIXELS : (group * 4 + tile + 1) * PIXELS] for tile in range(4)
        ]
        rows.append(jnp.concatenate(parts, axis=1))
    return jnp.concatenate(rows, axis=0)


def to_rows(x):
    groups = x.shape[0] // PIXELS
    parts = []
    for group in range(groups):
        for tile in range(4):
            parts.append(x[group * PIXELS : (group + 1) * PIXELS, tile * 128 : (tile + 1) * 128])
    return jnp.concatenate(parts, axis=0)


def taps_to_lanes(x):
    groups = x.shape[1] // 128
    rows = []
    for group in range(groups):
        parts = [
            x[tap * PIXELS : (tap + 1) * PIXELS, group * 128 : (group + 1) * 128]
            for tap in range(4)
        ]
        rows.append(jnp.concatenate(parts, axis=1))
    return jnp.concatenate(rows, axis=0)


def lanes_to_taps(x):
    groups = x.shape[0] // PIXELS
    columns = []
    for group in range(groups):
        parts = [
            x[group * PIXELS : (group + 1) * PIXELS, tap * 128 : (tap + 1) * 128]
            for tap in range(4)
        ]
        columns.append(jnp.concatenate(parts, axis=0))
    return jnp.concatenate(columns, axis=1)


def fill_select(select_s):
    row = lax.broadcasted_iota(jnp.int32, (256, 256), 0)
    column = lax.broadcasted_iota(jnp.int32, (256, 256), 1)
    tap, i, j = row // 64, row // 8 % 8, row % 8
    meet = column == 16 * (2 * i + tap // 2) + 2 * j + tap % 2
    select_s[...] = jnp.where(meet, 1.0, 0.0).astype(BF16)


def place_of(quad):
    return (1 - quad // 2) * 7, (1 - quad % 2) * 7


def corner(x, at):
    return jnp.broadcast_to(x[:, at : at + 1, :], x.shape)


def pack(parts):
    rows = parts[0].shape[0] * 8
    return jnp.concatenate([part.reshape(rows, 128).astype(BF16) for part in parts], axis=1)


def edges_of(edge_s, number):
    rows, cols = [], []
    for quad in range(4):
        at_y, at_x = place_of(quad)
        row = edge_s[0, quad, : number * 8, :].reshape(number, 8, 128)
        col = edge_s[1, quad, : number * 8, :].reshape(number, 8, 128)
        place = lax.broadcasted_iota(jnp.int32, row.shape, 1)
        rows.append(row)
        cols.append(jnp.where(place == at_y, corner(row, at_x), col))
    return rows, cols


def write_reply(reply_s, quad, row, col):
    at_y, at_x = place_of(quad)
    rows = row.shape[0] * 8
    place = lax.broadcasted_iota(jnp.int32, row.shape, 1)
    row = row + jnp.where(place == at_x, corner(col, at_y), 0.0)
    reply_s[0, quad, :rows, :] = row.reshape(rows, 128)
    reply_s[1, quad, :rows, :] = jnp.where(place == at_y, 0.0, col).reshape(rows, 128)


def fold_taps(acc):
    taps = []
    for tap in range(4):
        part = jnp.zeros((32, 128), F32)
        for tile in range(4):
            row = tap * 128 + tile * 32
            part += acc[row : row + 32, tile * 128 : (tile + 1) * 128]
        taps.append(part)
    return jnp.concatenate(taps, axis=0)


def rows_at(step, size):
    return pl.ds(pl.multiple_of(step * size, size), size)


def side_of(ref, tile):
    return jnp.broadcast_to(ref[pl.ds(tile, 1), :], (8, 128))


def read_edges(value_s, low_ref, right_ref, cell_ref, edges_s, step):
    place = lax.broadcasted_iota(jnp.int32, (8, 128), 0)
    for index in range(CHUNK):
        tile = step * CHUNK + index
        start = pl.multiple_of(tile * PIXELS, PIXELS)
        low, right = side_of(low_ref, tile), side_of(right_ref, tile)
        top = value_s[pl.ds(start, 8), :]
        bottom = value_s[pl.ds(start + 56, 8), :]
        left = value_s[pl.ds(start, 8, stride=8), :]
        end = value_s[pl.ds(start + 7, 8, stride=8), :]
        row = bottom * (1.0 - low) + top * low
        col = end * (1.0 - right) + left * right
        col = col * (1.0 - low) + pltpu.roll(col, 7, 0) * low
        if cell_ref is not None:
            col = jnp.where(place == 7, side_of(cell_ref, tile), col)
        at = pl.ds(pl.multiple_of(tile * EDGE_ROWS, EDGE_ROWS), EDGE_ROWS)
        edges_s[at, :] = jnp.concatenate([row, col], axis=0).astype(BF16)


def fill_holder_routes(owner_ref, hold_s, slots):
    columns = hold_s.shape[1]
    column = lax.broadcasted_iota(jnp.int32, (EDGE_ROWS, columns), 1)
    row = lax.broadcasted_iota(jnp.int32, (EDGE_ROWS, columns), 0)
    here = jnp.where(row == column % EDGE_ROWS, 1.0, 0.0)
    owner = jnp.broadcast_to(owner_ref[...], (EDGE_ROWS, columns))

    def one(slot, carry):
        at = pl.ds(pl.multiple_of(slot * EDGE_ROWS, EDGE_ROWS), EDGE_ROWS)
        hold_s[at, :] = jnp.where(owner == slot.astype(F32), here, 0.0).astype(BF16)
        return carry

    lax.fori_loop(0, slots, one, 0, unroll=2)


def fill_routes(got_ref, route_s):
    slots, columns = got_ref.shape[0], route_s.shape[1]
    column = lax.broadcasted_iota(jnp.int32, (EDGE_ROWS, columns), 1)
    row = lax.broadcasted_iota(jnp.int32, (EDGE_ROWS, columns), 0)
    kind, rest = column // (columns // 2), column % (columns // 2)
    quad, rest = rest // (columns // 8), rest % (columns // 8)
    tile, place = rest // 8, rest % 8
    turned = jnp.where((kind == 1) & (quad >= 2), (place + 7) % 8, place)
    here = jnp.where(row == kind * 8 + turned, 1.0, 0.0)
    cell = (tile * 4 + quad + 1).astype(F32)

    def one(slot, carry):
        tag = got_ref[slot].astype(F32)[EDGE_ROWS - 1 :]
        tag = jnp.concatenate([jnp.broadcast_to(tag, (EDGE_ROWS, 128))] * (columns // 128), axis=1)
        at = pl.ds(pl.multiple_of(slot * EDGE_ROWS, EDGE_ROWS), EDGE_ROWS)
        route_s[at, :] = jnp.where(tag == cell, here, 0.0).astype(BF16)
        return carry

    lax.fori_loop(0, slots, one, 0, unroll=2)


def gather_edges(route_s, got_ref, edge_s):
    rows = got_ref.shape[0] * EDGE_ROWS
    turned = mm_tn(got_ref[...].reshape(rows, 128), route_s[...])
    edge_s[...] = turned.T.reshape(edge_s.shape)


def scatter_edges(route_s, reply_s, send_ref):
    flat = reply_s[...].reshape(route_s.shape[1], 128).astype(BF16)
    send_ref[...] = mm(route_s[...], flat).astype(BF16).reshape(send_ref.shape)


def send_edges(hold_s, edges_s, send_ref):
    send_ref[...] = mm(hold_s[...], edges_s[...]).astype(BF16).reshape(send_ref.shape)


def take_reply(hold_s, got_ref, reply_in_s):
    rows = got_ref.shape[0] * EDGE_ROWS
    reply_in_s[...] = mm_tn(got_ref[...].reshape(rows, 128), hold_s[...]).T


def cross_mid(mid_ref, edge_s, act_edge_s, reply_s):
    number = edge_s.shape[2] // 8
    act_row, act_col = edges_of(edge_s, number)
    for quad in range(4):
        low, right = quad // 2, quad % 2
        act_edge_s[0, quad] = act_row[quad].reshape(number * 8, 128).astype(BF16)
        act_edge_s[1, quad] = act_col[quad].reshape(number * 8, 128).astype(BF16)
        across, beyond, beside = act_row[quad ^ 2], act_row[quad ^ 3], act_col[quad ^ 1]
        fills = [beyond if right == 1 else None, None, beyond if right == 0 else None]
        sy, sx = 2 - 2 * low, 2 - 2 * right
        patch = pack([shift8(across, s - 1, fills[s]) for s in range(3)])
        weight = jnp.concatenate([mid_ref[3 * sy + s] for s in range(3)], axis=0)
        row = mm(patch, weight).reshape(number, 8, 128)
        patch = pack([shift8(beside, s - 1) for s in range(3)])
        weight = jnp.concatenate([mid_ref[3 * s + sx] for s in range(3)], axis=0)
        col = mm(patch, weight).reshape(number, 8, 128)
        write_reply(reply_s, quad, row, col)


def cross_grad(mid_ref, edge_s, act_edge_s, reply_s, cross_ref):
    number = edge_s.shape[2] // 8
    grad_row, grad_col = edges_of(edge_s, number)
    for quad in range(4):
        low, right = quad // 2, quad % 2
        across, beyond, beside = grad_row[quad ^ 2], grad_row[quad ^ 3], grad_col[quad ^ 1]
        fills = [beyond if right == 0 else None, None, beyond if right == 1 else None]
        sy, sx = 2 * low, 2 * right
        patch = pack([shift8(across, 1 - s, fills[s]) for s in range(3)])
        weight = jnp.concatenate([mid_ref[3 * sy + s] for s in range(3)], axis=1)
        row = mm_nt(patch, weight).reshape(number, 8, 128)
        cross_ref[sy * 128 : (sy + 1) * 128, :] += mm_tn(act_edge_s[0, quad], patch)
        patch = pack([shift8(beside, 1 - s) for s in range(3)])
        weight = jnp.concatenate([mid_ref[3 * s + sx] for s in range(3)], axis=1)
        col = mm_nt(patch, weight).reshape(number, 8, 128)
        part = mm_tn(act_edge_s[1, quad], patch)
        for s in range(3):
            cross_ref[s * 128 : (s + 1) * 128, sx * 128 : (sx + 1) * 128] += (
                part[:, s * 128 : (s + 1) * 128]
            )
        write_reply(reply_s, quad, row, col)


def foreign(low_ref, right_ref, reply_in_s, step):
    place = lax.broadcasted_iota(jnp.int32, (8, 128), 0)
    parts = []
    for index in range(CHUNK):
        tile = step * CHUNK + index
        start = pl.multiple_of(tile * EDGE_ROWS, EDGE_ROWS)
        low, right = side_of(low_ref, tile), side_of(right_ref, tile)
        row = reply_in_s[pl.ds(start, 8), :]
        col = reply_in_s[pl.ds(start + 8, 8), :]
        col = col * (1.0 - low) + pltpu.roll(col, 1, 0) * low
        mask = jnp.where(place == 0, right, jnp.where(place == 7, 1.0 - right, 0.0))
        for i in range(8):
            part = mask * jnp.broadcast_to(col[i : i + 1], (8, 128))
            if i == 0:
                part += row * low
            elif i == 7:
                part += row * (1.0 - low)
            parts.append(part)
    return jnp.concatenate(parts, axis=0)


def block(
    events, plane, slots, pieces, scale,
    owner_ref, shown_ref, low_ref, right_ref, cell_ref, active_ref, fine_ref, cot_ref, down_ref, mid_ref, up_ref,
    grad_fine_ref, grad_down_ref, grad_mid_ref, grad_up_ref,
    select_s, down_s, up_s, conv_s, back_s, hold_s, edges_s, reply_in_s,
    x_s, g_s, pre_s, act_s, value_s, mid_s, grad_out_s, out_s,
    send0_s, send1_s, send2_s, send3_s, got0_s, got1_s, got2_s, got3_s, route_s, edge_s, act_edge_s, reply_s,
    mid_acc, up_acc, down_acc,
    mine_s, near_s, sum_s, far_s, fin_s, low_s, all_s,
    mine2_s, near2_s, low2_s, far2_s, fin2_s, all2_s,
    swap_send, swap_recv,
    near_send, near_recv, far_send, far_recv, fin_send, fin_recv, all_send, all_recv,
    near2_send, near2_recv, far2_send, far2_recv, all2_send, all2_recv,
):
    number = fine_ref.shape[0]
    steps = number // CHUNK
    step_rows = CHUNK * PIXELS
    event = lax.axis_index("event")
    tile_at = lax.axis_index("tile")
    z = tile_at // plane
    depth = slots // plane
    group = events * plane
    me = event * plane + tile_at % plane

    def near_id(p):
        return (p // plane, z * plane + p % plane)

    def far_id(p):
        return (event, p * plane + tile_at % plane)

    send_s = (send0_s, send1_s, send2_s, send3_s)
    got_s = (got0_s, got1_s, got2_s, got3_s)
    barrier = pltpu.get_barrier_semaphore()

    def greet(to):
        pl.semaphore_signal(barrier, inc=1, device_id=to, device_id_type=MESH)

    def greet_tile(k, carry):
        greet((event, (tile_at + k) % slots))
        return carry

    def greet_event(k, carry):
        other = (event + 1 + k // plane) % events
        greet((other, z * plane + k % plane))
        return carry

    def swap_copy(index, to):
        return pltpu.make_async_remote_copy(
            src_ref=send_s[index].at[to],
            dst_ref=got_s[index].at[tile_at],
            send_sem=swap_send.at[index],
            recv_sem=swap_recv.at[index],
            device_id=(event, to),
            device_id_type=MESH,
        )

    def swap_start(index):
        def one(k, carry):
            swap_copy(index, (tile_at + k) % slots).start()
            return carry

        lax.fori_loop(1, slots, one, 0)
        got_s[index][tile_at] = send_s[index][tile_at]

    def swap_all(index):
        some = pl.ds(0, slots - 1)
        return pltpu.make_async_remote_copy(
            src_ref=send_s[index].at[some],
            dst_ref=got_s[index].at[some],
            send_sem=swap_send.at[index],
            recv_sem=swap_recv.at[index],
            device_id=(event, (tile_at + 1) % slots),
            device_id_type=MESH,
        )

    lax.fori_loop(1, slots, greet_tile, 0)
    lax.fori_loop(0, group - plane, greet_event, 0)
    fill_select(select_s)
    spread_weight(down_ref, down_s)

    def down_step(step, carry):
        tiles = fine_ref[rows_at(step, CHUNK)].reshape(CHUNK * 32, 256)
        x_taps = taps_to_lanes(mm_nt(select_s[...], tiles).astype(BF16))
        x_s[rows_at(step, step_rows // 4), :] = x_taps
        pre = to_rows(mm(x_taps, down_s[...]))
        at = rows_at(step, step_rows)
        pre_s[at, :] = pre
        act = (pre * sigmoid(pre)).astype(BF16)
        act_s[at, :] = act
        value_s[at, :] = act.astype(F32)
        read_edges(value_s, low_ref, right_ref, cell_ref, edges_s, step)
        return carry

    lax.fori_loop(0, steps, down_step, 0)
    fill_holder_routes(owner_ref, hold_s, slots)
    send_edges(hold_s, edges_s, send0_s)
    pl.semaphore_wait(barrier, slots - 1 + group - plane)
    swap_start(0)

    spread_weight(up_ref, up_s)
    for sy in range(3):
        for sx in range(3):
            weight = mid_ref[3 * sy + sx]
            conv_s[sx * 128 : (sx + 1) * 128, sy * 128 : (sy + 1) * 128] = weight
            back_s[sy * 128 : (sy + 1) * 128, sx * 128 : (sx + 1) * 128] = weight
    mid_acc[...] = jnp.zeros_like(mid_acc)
    up_acc[...] = jnp.zeros_like(up_acc)
    down_acc[...] = jnp.zeros_like(down_acc)

    def local_step(step, carry):
        tiles = cot_ref[rows_at(step, CHUNK)].reshape(CHUNK * 32, 256)
        g_taps = mm_nt(select_s[...], tiles)
        g_taps = g_taps * shown_ref[:, rows_at(step, CHUNK * 32)]
        g_taps = taps_to_lanes(g_taps.astype(BF16))
        g_s[rows_at(step, step_rows // 4), :] = g_taps
        at = rows_at(step, step_rows)
        grad_out_s[at, :] = to_rows(mm(g_taps, up_s[...])).astype(BF16)
        parts = mm(side_steps(value_s[at, :], False), conv_s[...])
        mid_s[at, :] = (
            row_step(parts[:, :128], -1) + parts[:, 128:256] + row_step(parts[:, 256:], 1)
        )
        return carry

    lax.fori_loop(0, steps, local_step, 0)
    swap_all(0).wait_recv()

    fill_routes(got0_s, route_s)
    gather_edges(route_s, got0_s, edge_s)
    cross_mid(mid_ref, edge_s, act_edge_s, reply_s)
    scatter_edges(route_s, reply_s, send1_s)
    swap_start(1)
    swap_all(1).wait_recv()

    def slope_step(step, carry):
        at = rows_at(step, step_rows)
        mid = mid_s[at, :] + foreign(low_ref, right_ref, reply_in_s, step)
        gate = sigmoid(mid)
        out_s[at, :] = (act_s[at, :].astype(F32) + mid * gate).astype(BF16)
        grad = grad_out_s[at, :].astype(F32) * (gate * (1.0 + mid * (1.0 - gate)))
        value_s[at, :] = grad.astype(BF16).astype(F32)
        read_edges(value_s, low_ref, right_ref, None, edges_s, step)
        return carry

    take_reply(hold_s, got1_s, reply_in_s)
    lax.fori_loop(0, steps, slope_step, 0)
    send_edges(hold_s, edges_s, send2_s)
    swap_start(2)

    def grad_step(step, carry):
        at = rows_at(step, step_rows)
        up_acc[...] += mm_tn(g_s[rows_at(step, step_rows // 4), :], to_lanes(out_s[at, :]))
        steps_of = side_steps(value_s[at, :], True)
        parts = mm_nt(steps_of, back_s[...])
        mid_s[at, :] = (
            grad_out_s[at, :].astype(F32)
            + row_step(parts[:, :128], 1)
            + parts[:, 128:256]
            + row_step(parts[:, 256:], -1)
        )
        act = act_s[at, :].astype(F32)
        acts = jnp.concatenate([row_step(act, s - 1).astype(BF16) for s in range(3)], axis=1)
        mid_acc[...] += mm_tn(acts, steps_of)
        return carry

    lax.fori_loop(0, steps, grad_step, 0)
    swap_all(2).wait_recv()

    gather_edges(route_s, got2_s, edge_s)
    cross_grad(mid_ref, edge_s, act_edge_s, reply_s, mid_acc)
    scatter_edges(route_s, reply_s, send3_s)
    swap_start(3)

    share = mine_s.shape[0] // group
    piece = share // pieces
    for tap in range(9):
        mine_s[tap * 128 : (tap + 1) * 128, :] = (
            mid_acc[
                tap // 3 * 128 : tap // 3 * 128 + 128, tap % 3 * 128 : tap % 3 * 128 + 128
            ]
            * scale
        ).astype(BF16)
    mine_s[1152:1280, :] = (fold_taps(up_acc) * scale).astype(BF16)
    if mine_s.shape[0] > 1280:
        mine_s[1280:, :] = jnp.zeros((mine_s.shape[0] - 1280, 128), BF16)

    def share_at(p):
        return pl.ds(pl.multiple_of(p * share, 16), share)

    def near_copy(to, slot):
        return pltpu.make_async_remote_copy(
            src_ref=mine_s.at[share_at(to)],
            dst_ref=near_s.at[slot],
            send_sem=near_send.at[to],
            recv_sem=near_recv.at[slot],
            device_id=near_id(to),
            device_id_type=MESH,
        )

    def far_copy(to, slot):
        return pltpu.make_async_remote_copy(
            src_ref=sum_s.at[to],
            dst_ref=far_s.at[slot],
            send_sem=far_send.at[to],
            recv_sem=far_recv.at[slot],
            device_id=far_id(to),
            device_id_type=MESH,
        )

    def fin_copy(to, slot):
        return pltpu.make_async_remote_copy(
            src_ref=fin_s.at[slot],
            dst_ref=fin_s.at[slot],
            send_sem=fin_send.at[to],
            recv_sem=fin_recv.at[slot],
            device_id=far_id(to),
            device_id_type=MESH,
        )

    def all_copy(to, slot):
        return pltpu.make_async_remote_copy(
            src_ref=low_s,
            dst_ref=all_s.at[share_at(slot)],
            send_sem=all_send.at[to],
            recv_sem=all_recv.at[slot],
            device_id=near_id(to),
            device_id_type=MESH,
        )

    def each(first, last, body):
        def one(k, carry):
            body(k)
            return carry

        lax.fori_loop(first, last, one, 0)

    each(1, group, lambda k: near_copy((me + k) % group, me).start())

    def take_near(k, total):
        p = (me + k) % group
        near_copy(p, p).wait_recv()
        return total + near_s[p].astype(F32)

    total = lax.fori_loop(1, group, take_near, mine_s[share_at(me), :].astype(F32))
    sum_s[...] = total.reshape(pieces, piece, 128)
    for to in range(pieces):

        @pl.when(z != to)
        def _():
            far_copy(to, z).start()

    @pl.when(z < pieces)
    def _():
        def take_far(k, total):
            p = (z + k) % depth
            far_copy(z, p).wait_recv()
            return total + far_s[p]

        fin_s[z] = lax.fori_loop(1, depth, take_far, sum_s[z])
        each(1, depth, lambda k: fin_copy((z + k) % depth, z).start())

    for p in range(pieces):

        @pl.when(z != p)
        def _():
            fin_copy(p, p).wait_recv()

    low_s[...] = fin_s[...].reshape(share, 128).astype(BF16)
    each(1, group, lambda k: all_copy((me + k) % group, me).start())
    all_s[share_at(me), :] = low_s[...]

    swap_all(3).wait_recv()

    def pre_step(step, carry):
        at = rows_at(step, step_rows)
        grad_act = mid_s[at, :] + foreign(low_ref, right_ref, reply_in_s, step)
        grad_act = grad_act.astype(BF16).astype(F32)
        grad_pre = to_lanes((grad_act * slope(pre_s[at, :])).astype(BF16))
        lanes_at = rows_at(step, step_rows // 4)
        down_acc[...] += mm_tn(x_s[lanes_at, :], grad_pre)
        g_s[lanes_at, :] = grad_pre
        return carry

    take_reply(hold_s, got3_s, reply_in_s)
    lax.fori_loop(0, steps, pre_step, 0)
    parts = mine2_s.shape[0]
    stride = group // parts
    my_part = me // stride
    reducer = me % stride == 0
    mine2_s[...] = (fold_taps(down_acc) * scale).astype(BF16).reshape(mine2_s.shape)

    def near2_copy(part, slot):
        return pltpu.make_async_remote_copy(
            src_ref=mine2_s.at[part],
            dst_ref=near2_s.at[slot],
            send_sem=near2_send.at[part],
            recv_sem=near2_recv.at[slot],
            device_id=near_id(part * stride),
            device_id_type=MESH,
        )

    def far2_copy(to, slot):
        return pltpu.make_async_remote_copy(
            src_ref=low2_s,
            dst_ref=far2_s.at[slot],
            send_sem=far2_send.at[to],
            recv_sem=far2_recv.at[slot],
            device_id=far_id(to),
            device_id_type=MESH,
        )

    def all2_copy(to, part):
        return pltpu.make_async_remote_copy(
            src_ref=fin2_s,
            dst_ref=all2_s.at[part],
            send_sem=all2_send.at[to],
            recv_sem=all2_recv.at[part],
            device_id=near_id(to),
            device_id_type=MESH,
        )

    for part in range(parts):

        @pl.when(me != part * stride)
        def _():
            near2_copy(part, me).start()

    def fine_step(step, carry):
        back = lanes_to_taps(mm_nt(g_s[rows_at(step, step_rows // 4), :], down_s[...]))
        high = back.astype(BF16)
        rest = (back - high.astype(F32)).astype(BF16)
        select = select_s[...]
        total = mm_tn(high, select) + mm_tn(rest, select)
        total += cot_ref[rows_at(step, CHUNK)].reshape(CHUNK * 32, 256).astype(F32)
        shown = [
            jnp.broadcast_to(active_ref[pl.ds(step * CHUNK + index, 1), :], (32, 128))
            for index in range(CHUNK)
        ]
        shown = jnp.concatenate(shown, axis=0)
        total = total * jnp.concatenate([shown, shown], axis=1)
        grad_fine_ref[rows_at(step, CHUNK)] = total.astype(BF16).reshape(CHUNK, 32, 256)
        return carry

    first, second = steps * 2 // 5, steps * 4 // 5
    lax.fori_loop(0, first, fine_step, 0)

    @pl.when(reducer)
    def _():
        def take(k, total):
            p = (me + k) % group
            near2_copy(my_part, p).wait_recv()
            return total + near2_s[p].astype(F32)

        low2_s[...] = lax.fori_loop(1, group, take, mine2_s[my_part].astype(F32)).astype(BF16)
        each(1, depth, lambda k: far2_copy((z + k) % depth, z).start())
        far2_s[z] = low2_s[...]

    lax.fori_loop(first, second, fine_step, 0)

    @pl.when(reducer)
    def _():
        def take(k):
            p = (z + k) % depth
            far2_copy(p, p).wait_recv()

        each(1, depth, take)
        fin2_s[...] = jnp.sum(far2_s[...].astype(F32), axis=0).astype(BF16)
        each(1, group, lambda k: all2_copy((me + k) % group, my_part).start())
        all2_s[my_part] = fin2_s[...]

    lax.fori_loop(second, steps, fine_step, 0)

    def take_all(k):
        p = (me + k) % group
        all_copy(p, p).wait_recv()

    each(1, group, take_all)
    grad_mid_ref[...] = all_s[:1152, :].astype(F32)
    grad_up_ref[...] = all_s[1152:1280, :].astype(F32)

    for index in range(4):
        swap_all(index).wait_send()

    def sent_near(k):
        p = (me + k) % group
        near_copy(p, me).wait_send()
        all_copy(p, me).wait_send()

    each(1, group, sent_near)
    for to in range(pieces):

        @pl.when(z != to)
        def _():
            far_copy(to, z).wait_send()

    @pl.when(z < pieces)
    def _():
        each(1, depth, lambda k: fin_copy((z + k) % depth, z).wait_send())

    for part in range(parts):

        @pl.when(me != part * stride)
        def _():
            near2_copy(part, me).wait_send()
            all2_copy(me, part).wait_recv()

    grad_down_ref[...] = all2_s[...].reshape(grad_down_ref.shape).astype(F32)

    @pl.when(reducer)
    def _():
        each(1, depth, lambda k: far2_copy((z + k) % depth, z).wait_send())
        each(1, group, lambda k: all2_copy((me + k) % group, my_part).wait_send())


def like(shape, dtype):
    return jax.ShapeDtypeStruct(shape, dtype)


def shards(plane, fine, cotangent, counts, parent, quadrant, down_weight, mid_weight, up_weight):
    number = fine.shape[1]
    slots = lax.axis_size("tile")
    events = lax.axis_size("event")
    coarse_dev = number // 4
    rows = number * PIXELS
    scale = 1.0 / math.sqrt(events * slots * number * 64)

    active = jnp.arange(number, dtype=jnp.int32) < counts[0, 0]
    shown = active.astype(F32)
    owner = jnp.where(active, parent[0] // coarse_dev, -1).astype(F32)
    cell = (parent[0] % coarse_dev * 4 + quadrant[0] + 1).astype(F32)
    low, right = (quadrant[0] // 2).astype(F32), (quadrant[0] % 2).astype(F32)

    def along(values, size):
        return jnp.broadcast_to(values[:, None], (number, size)).reshape(1, number * size)

    def across(values):
        return jnp.broadcast_to(values[:, None], (number, 128))

    places = (
        along(owner, EDGE_ROWS), along(shown, 32),
        across(low), across(right), across(cell), across(shown),
    )

    group = events * plane
    depth = slots // plane
    share = -(-1280 // (group * 16)) * 16
    pieces = max(n for n in range(1, share // 8 + 1) if share // 8 % n == 0 and n <= depth)
    piece = share // pieces
    dma = pltpu.SemaphoreType.DMA
    vm = pltpu.VMEM
    vmem = pl.BlockSpec(memory_space=vm)
    grad_fine, grad_down, grad_mid, grad_up = pl.pallas_call(
        functools.partial(block, events, plane, slots, pieces, scale),
        in_specs=[vmem] * 11,
        out_specs=[vmem] * 4,
        out_shape=[
            like((number, 32, 256), BF16),
            like((128, 128), F32),
            like((1152, 128), F32),
            like((128, 128), F32),
        ],
        scratch_shapes=[
            vm((256, 256), BF16),
            vm((512, 512), BF16),
            vm((512, 512), BF16),
            vm((384, 384), BF16),
            vm((384, 384), BF16),
            vm((slots * EDGE_ROWS, number * EDGE_ROWS), BF16),
            vm((number * EDGE_ROWS, 128), BF16),
            vm((number * EDGE_ROWS, 128), F32),
            vm((rows // 4, 512), BF16),
            vm((rows // 4, 512), BF16),
            vm((rows, 128), F32),
            vm((rows, 128), BF16),
            vm((rows, 128), F32),
            vm((rows, 128), F32),
            vm((rows, 128), BF16),
            vm((rows, 128), BF16),
            *[vm((slots, EDGE_ROWS, 128), BF16) for _ in range(8)],
            vm((slots * EDGE_ROWS, number * EDGE_ROWS), BF16),
            vm((2, 4, number * 2, 128), F32),
            vm((2, 4, number * 2, 128), BF16),
            vm((2, 4, number * 2, 128), F32),
            vm((384, 384), F32),
            vm((512, 512), F32),
            vm((512, 512), F32),
            vm((group * share, 128), BF16),
            vm((group, share, 128), BF16),
            vm((pieces, piece, 128), F32),
            vm((depth, piece, 128), F32),
            vm((pieces, piece, 128), F32),
            vm((share, 128), BF16),
            vm((group * share, 128), BF16),
            vm((8, 16, 128), BF16),
            vm((group, 16, 128), BF16),
            vm((16, 128), BF16),
            vm((depth, 16, 128), BF16),
            vm((16, 128), BF16),
            vm((8, 16, 128), BF16),
            dma((4,)),
            dma((4,)),
            dma((group,)),
            dma((group,)),
            dma((pieces,)),
            dma((depth,)),
            dma((depth,)),
            dma((pieces,)),
            dma((group,)),
            dma((group,)),
            dma((8,)),
            dma((group,)),
            dma((depth,)),
            dma((depth,)),
            dma((group,)),
            dma((8,)),
        ],
        compiler_params=pltpu.CompilerParams(
            collective_id=0, has_side_effects=True, vmem_limit_bytes=VMEM_LIMIT
        ),
        name="residual_block",
    )(*places, fine[0], cotangent[0], down_weight, mid_weight, up_weight)
    return (
        grad_fine[None],
        grad_down.reshape(4, 32, 128),
        grad_mid.reshape(9, 128, 128),
        grad_up.reshape(4, 32, 128),
    )


def solution(mesh):
    placed = (
        P("event", "tile", None, None),
        P("event", "tile", None, None),
        P("event", "tile"),
        P("event", "tile"),
        P("event", "tile"),
        P(),
        P(),
        P(),
    )
    return jax.shard_map(
        functools.partial(shards, 8),
        mesh=mesh,
        in_specs=placed,
        out_specs=(P("event", "tile", None, None), P(), P(), P()),
        check_vma=False,
    )
```

time: 907 us -> 200 us (0.22)
  waiting for transfers between devices: 581 us -> 0 us
  Pallas kernels: 0 us -> 189 us
  blocking collectives: 106 us -> 0 us
  local copies, waits for them, and re-layouts: 106 us -> 8.91 us
  starting transfers between devices: 42 us -> 0 us
  matrix products: 30.3 us -> 0 us
  other arithmetic: 19.5 us -> 0.7 us
  between operations: 15.6 us -> 1.32 us
    psum x1 -> x0, waiting for transfers between devices: 398 us -> none  [shards(): lax.psum((grad_down * grad_scale, grad_mid * grad_scale, grad_up * grad_s...]
    pallas_call x0 -> x1, Pallas kernels: none -> 189 us  [shards(): pl.pallas_call(functools.partial(block, events, plane, slots, pieces, sca...]
    all_to_all x3 -> x0, waiting for transfers between devices: 183 us -> none  [the longest x1 89.8 us: shards(): lax.all_to_all(cot_send, 'tile', split_axis=0, concat_axis=0, tiled=True)]
    all_to_all x1 -> x0, blocking collectives: 106 us -> none  [shards(): lax.all_to_all(lead_send, 'tile', split_axis=0, concat_axis=0, tiled=True)]
    all_to_all x3 -> x0, starting transfers between devices: 41.9 us -> none  [the longest x1 20.6 us: shards(): lax.all_to_all(cell_tags, 'tile', split_axis=0, concat_axis=0, tiled=True)]
    dot_general x8 -> x0, matrix products: 30.3 us -> none  [the longest x1 9.46 us: shards(): mid_pre = jnp.dot(act_patch, mid_flat, preferred_element_type=jnp.float32)]
    transpose x3 -> x0, local copies, waits for them, and re-layouts: 29.7 us -> none  [the longest x2 20.7 us: split_taps(): return blocks.transpose(0, 2, 4, 3, 5, 1).reshape(number, 64, 4 * channels)]
    another operation x4 -> x0, local copies, waits for them, and re-layouts: 22.2 us -> none  [the longest x1 10.4 us: shards(): child_taps = split_taps(lead_quads).reshape(-1, 4 * fine_ch)]
  transfers between devices with their start and end apart: 4 -> 0, of which waited for: 4 -> 0; matrix products, arithmetic and copies ran while one was open for 3% -> 0% of each run, Pallas kernels for 0% -> 0%
where the time goes in v3:
time: 200 us
  Pallas kernels  189 us (94%)
  local copies, waits for them, and re-layouts  8.91 us (4%)
    pallas_call x1, Pallas kernels, shards(): pl.pallas_call(functools.partial(block, events, plane, slots, pieces, sca...  189 us
    unnamed x10, local copies, waits for them, and re-layouts  4.62 us

profile of v3, /device:TPU:1, one launch (start us, length us, event | category | flops | bytes accessed | tf_op | source)
XLA Modules:
  0.0 200.0 jit_solution(14239422135152131746)
XLA Ops:
  1.3 0.7 add_convert_fusion
  2.0 0.7 broadcast_in_dim.20.cell_ref
  2.7 0.1 broadcast_in_dim.16
  2.7 0.7 reshape.123.owner_ref
  3.4 0.7 broadcast_in_dim.18.low_ref
  4.1 0.7 broadcast_in_dim.19.right_ref
  4.8 0.7 broadcast_in_dim.21.active_ref
  5.5 0.1 broadcast_in_dim.17
  5.6 0.7 reshape.124.shown_ref
  6.3 189.0 %residual_block.1 = (bf16[80,32,256]{2,1,0:T(8,128)(2,1)}, f32[128,128]{1,0:T(8,128)}, f32[1152,128]{1,0:T(8,128)}, f32[128,128]{1,0:T(8,128)}) custom-call(f32[1,1280]{1,0:T(1,128)} %reshape.123.owner_ref, f32[1,2560]{1,0:T(1,128)} %reshape.124.shown_ref, f32[80,128]{1,0:T(8,128)} %broadcast_in_dim.18.low_ref, f32[80,128]{1,0:T(8,128)} %broadcast_in_dim.19.right_ref, ...), custom_call_target="tpu_custom_call" | custom-call | tf_op jit(solution)/shard_map/residual_block/pallas_call | solution.py:771
  195.3 0.0 copy-start.2
  195.3 0.0 copy-start
  195.3 2.5 %copy.17 = bf16[1,80,32,256]{3,2,1,0:T(8,128)(2,1)} copy(bf16[1,80,32,256]{3,2,1,0:T(8,128)(2,1)} %bitcast.48) | data formatting | bytes 2621440
  197.9 0.0 copy-done.2
  197.9 0.0 copy-start.1
  197.9 0.6 copy.18
  198.5 0.0 copy-done
  198.5 0.8 copy.19
  199.3 0.0 copy-done.1
  199.3 0.6 copy.20
  (1 shorter events, 0.0 us)
Async XLA Ops:
  195.3 2.6 %copy-start.2 = (f32[128,128]{1,0:T(8,128)S(1)}, f32[128,128]{1,0:T(8,128)}, u32[]{:S(2)}) copy-start(f32[128,128]{1,0:T(8,128)} %get-tuple-element.9) | copy-start | bytes 196612
  195.3 3.2 %copy-start = (f32[1152,128]{1,0:T(8,128)S(1)}, f32[1152,128]{1,0:T(8,128)}, u32[]{:S(2)}) copy-start(f32[1152,128]{1,0:T(8,128)} %get-tuple-element.10) | copy-start | bytes 1769476
  197.9 1.5 copy-start.1

commit v4 on v3

--- a/solution.py
+++ b/solution.py
@@ -204,7 +204,7 @@
     column = lax.broadcasted_iota(jnp.int32, (EDGE_ROWS, columns), 1)
     row = lax.broadcasted_iota(jnp.int32, (EDGE_ROWS, columns), 0)
     here = jnp.where(row == column % EDGE_ROWS, 1.0, 0.0)
-    owner = jnp.broadcast_to(owner_ref[...], (EDGE_ROWS, columns))
+    owner = jnp.broadcast_to(owner_ref[0:1, :], (EDGE_ROWS, columns))
 
     def one(slot, carry):
         at = pl.ds(pl.multiple_of(slot * EDGE_ROWS, EDGE_ROWS), EDGE_ROWS)
@@ -318,17 +318,30 @@
     return jnp.concatenate(parts, axis=0)
 
 
+def spread_places(place_ref, owner_s, shown_s, across):
+    places = place_ref[...].astype(BF16)
+    lanes = places.shape[1]
+    for target, size in ((owner_s, EDGE_ROWS), (shown_s, 32)):
+        row = lax.broadcasted_iota(jnp.int32, (lanes, target.shape[1]), 0)
+        column = lax.broadcasted_iota(jnp.int32, (lanes, target.shape[1]), 1)
+        target[...] = mm(places, jnp.where(column // size == row, 1.0, 0.0).astype(BF16))
+    place = lax.broadcasted_iota(jnp.int32, (16, 128), 0)
+    for index, target in enumerate(across):
+        target[...] = mm_tn(places, jnp.where(place == index + 1, 1.0, 0.0).astype(BF16))
+
+
 def block(
     events, plane, slots, pieces, scale,
-    owner_ref, shown_ref, low_ref, right_ref, cell_ref, active_ref, fine_ref, cot_ref, down_ref, mid_ref, up_ref,
+    place_ref, fine_hbm, cot_hbm, down_hbm, mid_hbm, up_hbm,
     grad_fine_ref, grad_down_ref, grad_mid_ref, grad_up_ref,
-    select_s, down_s, up_s, conv_s, back_s, hold_s, edges_s, reply_in_s,
+    select_s, down_s, up_s, fine_ref, cot_ref, down_ref, mid_ref, up_ref,
+    conv_s, back_s, owner_s, shown_s, low_s, right_s, cell_s, active_s, hold_s, edges_s, reply_in_s,
     x_s, g_s, pre_s, act_s, value_s, mid_s, grad_out_s, out_s,
     send0_s, send1_s, send2_s, send3_s, got0_s, got1_s, got2_s, got3_s, route_s, edge_s, act_edge_s, reply_s,
     mid_acc, up_acc, down_acc,
-    mine_s, near_s, sum_s, far_s, fin_s, low_s, all_s,
+    mine_s, near_s, sum_s, far_s, fin_s, half_s, all_s,
     mine2_s, near2_s, low2_s, far2_s, fin2_s, all2_s,
-    swap_send, swap_recv,
+    load_sem, swap_send, swap_recv,
     near_send, near_recv, far_send, far_recv, fin_send, fin_recv, all_send, all_recv,
     near2_send, near2_recv, far2_send, far2_recv, all2_send, all2_recv,
 ):
@@ -350,6 +363,20 @@
 
     send_s = (send0_s, send1_s, send2_s, send3_s)
     got_s = (got0_s, got1_s, got2_s, got3_s)
+    loads = [
+        pltpu.make_async_copy(source, target, load_sem.at[index])
+        for index, (source, target) in enumerate(
+            (
+                (fine_hbm, fine_ref),
+                (down_hbm, down_ref),
+                (cot_hbm, cot_ref),
+                (up_hbm, up_ref),
+                (mid_hbm, mid_ref),
+            )
+        )
+    ]
+    for load in loads:
+        load.start()
     barrier = pltpu.get_barrier_semaphore()
 
     def greet(to):
@@ -393,12 +420,22 @@
             device_id_type=MESH,
         )
 
-    lax.fori_loop(1, slots, greet_tile, 0)
-    lax.fori_loop(0, group - plane, greet_event, 0)
+    per_tile, per_event = (slots - 1) // steps, (group - plane) // steps
+    for k in range(1 + per_tile * steps, slots):
+        greet_tile(k, 0)
+    for k in range(per_event * steps, group - plane):
+        greet_event(k, 0)
+    spread_places(place_ref, owner_s, shown_s, (low_s, right_s, cell_s, active_s))
     fill_select(select_s)
+    loads[0].wait()
+    loads[1].wait()
     spread_weight(down_ref, down_s)
 
     def down_step(step, carry):
+        for k in range(per_tile):
+            greet_tile(1 + step * per_tile + k, 0)
+        for k in range(per_event):
+            greet_event(step * per_event + k, 0)
         tiles = fine_ref[rows_at(step, CHUNK)].reshape(CHUNK * 32, 256)
         x_taps = taps_to_lanes(mm_nt(select_s[...], tiles).astype(BF16))
         x_s[rows_at(step, step_rows // 4), :] = x_taps
@@ -408,15 +445,17 @@
         act = (pre * sigmoid(pre)).astype(BF16)
         act_s[at, :] = act
         value_s[at, :] = act.astype(F32)
-        read_edges(value_s, low_ref, right_ref, cell_ref, edges_s, step)
+        read_edges(value_s, low_s, right_s, cell_s, edges_s, step)
         return carry
 
     lax.fori_loop(0, steps, down_step, 0)
-    fill_holder_routes(owner_ref, hold_s, slots)
+    fill_holder_routes(owner_s, hold_s, slots)
     send_edges(hold_s, edges_s, send0_s)
     pl.semaphore_wait(barrier, slots - 1 + group - plane)
     swap_start(0)
 
+    for load in loads[2:]:
+        load.wait()
     spread_weight(up_ref, up_s)
     for sy in range(3):
         for sx in range(3):
@@ -430,7 +469,7 @@
     def local_step(step, carry):
         tiles = cot_ref[rows_at(step, CHUNK)].reshape(CHUNK * 32, 256)
         g_taps = mm_nt(select_s[...], tiles)
-        g_taps = g_taps * shown_ref[:, rows_at(step, CHUNK * 32)]
+        g_taps = g_taps * shown_s[4:5, rows_at(step, CHUNK * 32)]
         g_taps = taps_to_lanes(g_taps.astype(BF16))
         g_s[rows_at(step, step_rows // 4), :] = g_taps
         at = rows_at(step, step_rows)
@@ -453,12 +492,12 @@
 
     def slope_step(step, carry):
         at = rows_at(step, step_rows)
-        mid = mid_s[at, :] + foreign(low_ref, right_ref, reply_in_s, step)
+        mid = mid_s[at, :] + foreign(low_s, right_s, reply_in_s, step)
         gate = sigmoid(mid)
         out_s[at, :] = (act_s[at, :].astype(F32) + mid * gate).astype(BF16)
         grad = grad_out_s[at, :].astype(F32) * (gate * (1.0 + mid * (1.0 - gate)))
         value_s[at, :] = grad.astype(BF16).astype(F32)
-        read_edges(value_s, low_ref, right_ref, None, edges_s, step)
+        read_edges(value_s, low_s, right_s, None, edges_s, step)
         return carry
 
     take_reply(hold_s, got1_s, reply_in_s)
@@ -538,7 +577,7 @@
 
     def all_copy(to, slot):
         return pltpu.make_async_remote_copy(
-            src_ref=low_s,
+            src_ref=half_s,
             dst_ref=all_s.at[share_at(slot)],
             send_sem=all_send.at[to],
             recv_sem=all_recv.at[slot],
@@ -578,21 +617,11 @@
         fin_s[z] = lax.fori_loop(1, depth, take_far, sum_s[z])
         each(1, depth, lambda k: fin_copy((z + k) % depth, z).start())
 
-    for p in range(pieces):
-
-        @pl.when(z != p)
-        def _():
-            fin_copy(p, p).wait_recv()
-
-    low_s[...] = fin_s[...].reshape(share, 128).astype(BF16)
-    each(1, group, lambda k: all_copy((me + k) % group, me).start())
-    all_s[share_at(me), :] = low_s[...]
-
     swap_all(3).wait_recv()
 
     def pre_step(step, carry):
         at = rows_at(step, step_rows)
-        grad_act = mid_s[at, :] + foreign(low_ref, right_ref, reply_in_s, step)
+        grad_act = mid_s[at, :] + foreign(low_s, right_s, reply_in_s, step)
         grad_act = grad_act.astype(BF16).astype(F32)
         grad_pre = to_lanes((grad_act * slope(pre_s[at, :])).astype(BF16))
         lanes_at = rows_at(step, step_rows // 4)
@@ -644,6 +673,16 @@
         def _():
             near2_copy(part, me).start()
 
+    for p in range(pieces):
+
+        @pl.when(z != p)
+        def _():
+            fin_copy(p, p).wait_recv()
+
+    half_s[...] = fin_s[...].reshape(share, 128).astype(BF16)
+    each(1, group, lambda k: all_copy((me + k) % group, me).start())
+    all_s[share_at(me), :] = half_s[...]
+
     def fine_step(step, carry):
         back = lanes_to_taps(mm_nt(g_s[rows_at(step, step_rows // 4), :], down_s[...]))
         high = back.astype(BF16)
@@ -652,7 +691,7 @@
         total = mm_tn(high, select) + mm_tn(rest, select)
         total += cot_ref[rows_at(step, CHUNK)].reshape(CHUNK * 32, 256).astype(F32)
         shown = [
-            jnp.broadcast_to(active_ref[pl.ds(step * CHUNK + index, 1), :], (32, 128))
+            jnp.broadcast_to(active_s[pl.ds(step * CHUNK + index, 1), :], (32, 128))
             for index in range(CHUNK)
         ]
         shown = jnp.concatenate(shown, axis=0)
@@ -749,16 +788,9 @@
     cell = (parent[0] % coarse_dev * 4 + quadrant[0] + 1).astype(F32)
     low, right = (quadrant[0] // 2).astype(F32), (quadrant[0] % 2).astype(F32)
 
-    def along(values, size):
-        return jnp.broadcast_to(values[:, None], (number, size)).reshape(1, number * size)
-
-    def across(values):
-        return jnp.broadcast_to(values[:, None], (number, 128))
-
-    places = (
-        along(owner, EDGE_ROWS), along(shown, 32),
-        across(low), across(right), across(cell), across(shown),
-    )
+    lanes = -(-number // 128) * 128
+    places = jnp.stack([owner, low, right, cell, shown])
+    places = jnp.pad(places, ((0, 11), (0, lanes - number)))
 
     group = events * plane
     depth = slots // plane
@@ -770,7 +802,7 @@
     vmem = pl.BlockSpec(memory_space=vm)
     grad_fine, grad_down, grad_mid, grad_up = pl.pallas_call(
         functools.partial(block, events, plane, slots, pieces, scale),
-        in_specs=[vmem] * 11,
+        in_specs=[vmem] + [pl.BlockSpec(memory_space=pltpu.HBM)] * 5,
         out_specs=[vmem] * 4,
         out_shape=[
             like((number, 32, 256), BF16),
@@ -782,8 +814,16 @@
             vm((256, 256), BF16),
             vm((512, 512), BF16),
             vm((512, 512), BF16),
+            vm((number, 32, 256), BF16),
+            vm((number, 32, 256), BF16),
+            vm((4, 32, 128), BF16),
+            vm((9, 128, 128), BF16),
+            vm((4, 32, 128), BF16),
             vm((384, 384), BF16),
             vm((384, 384), BF16),
+            vm((16, number * EDGE_ROWS), F32),
+            vm((16, number * 32), F32),
+            *[vm((lanes, 128), F32) for _ in range(4)],
             vm((slots * EDGE_ROWS, number * EDGE_ROWS), BF16),
             vm((number * EDGE_ROWS, 128), BF16),
             vm((number * EDGE_ROWS, 128), F32),
@@ -791,7 +831,7 @@
             vm((rows // 4, 512), BF16),
             vm((rows, 128), F32),
             vm((rows, 128), BF16),
-            vm((rows, 128), F32),
+            vm((rows + 8, 128), F32),
             vm((rows, 128), F32),
             vm((rows, 128), BF16),
             vm((rows, 128), BF16),
@@ -816,6 +856,7 @@
             vm((depth, 16, 128), BF16),
             vm((16, 128), BF16),
             vm((8, 16, 128), BF16),
+            dma((5,)),
             dma((4,)),
             dma((4,)),
             dma((group,)),
@@ -837,7 +878,7 @@
             collective_id=0, has_side_effects=True, vmem_limit_bytes=VMEM_LIMIT
         ),
         name="residual_block",
-    )(*places, fine[0], cotangent[0], down_weight, mid_weight, up_weight)
+    )(places, fine[0], cotangent[0], down_weight, mid_weight, up_weight)
     return (
         grad_fine[None],
         grad_down.reshape(4, 32, 128),

time: 200 us -> 189 us (0.945)
  Pallas kernels: 189 us -> 181 us
  local copies, waits for them, and re-layouts: 8.91 us -> 5.25 us
    pallas_call x1, Pallas kernels: 189 us -> 181 us  [shards(): pl.pallas_call(functools.partial(block, events, plane, slots, pieces, sca...]
    broadcast_in_dim x6 -> x0, local copies, waits for them, and re-layouts: 2.92 us -> none  [the longest x4 2.77 us: across(): return jnp.broadcast_to(values[:, None], (number, 128))]
where the time goes in v4:
time: 189 us
  Pallas kernels  181 us (96%)
  local copies, waits for them, and re-layouts  5.25 us (3%)
    pallas_call x1, Pallas kernels, shards(): pl.pallas_call(functools.partial(block, events, plane, slots, pieces, sca...  181 us
    unnamed x10, local copies, waits for them, and re-layouts  4.62 us

profile of v4, /device:TPU:1, one launch (start us, length us, event | category | flops | bytes accessed | tf_op | source)
XLA Modules:
  0.0 188.5 jit_solution(16615063286742260113)
XLA Ops:
  1.3 0.7 add_convert_fusion
  2.0 0.6 pad.4.place_ref
  2.6 181.3 %residual_block.1 = (bf16[80,32,256]{2,1,0:T(8,128)(2,1)}, f32[128,128]{1,0:T(8,128)}, f32[1152,128]{1,0:T(8,128)}, f32[128,128]{1,0:T(8,128)}) custom-call(f32[16,128]{1,0:T(8,128)} %pad.4.place_ref, bf16[80,32,256]{2,1,0:T(8,128)(2,1)} %bitcast.9, bf16[80,32,256]{2,1,0:T(8,128)(2,1)} %bitcast.10, bf16[4,32,128]{2,1,0:T(8,128)(2,1)} %down_hbm.1, ...), custom_call_target="tpu_custom_call" | custom-call | tf_op jit(solution)/shard_map/residual_block/pallas_call | solution.py:803
  183.9 0.0 copy-start.2
  183.9 0.0 copy-start
  183.9 0.0 copy-start.1
  183.9 2.5 %copy.17 = bf16[1,80,32,256]{3,2,1,0:T(8,128)(2,1)} copy(bf16[1,80,32,256]{3,2,1,0:T(8,128)(2,1)} %bitcast.11) | data formatting | bytes 2621440
  186.5 0.0 copy-done.2
  186.5 0.6 copy.18
  187.1 0.0 copy-done
  187.1 0.8 copy.19
  187.9 0.0 copy-done.1
  187.9 0.6 copy.20
  (2 shorter events, 0.0 us)
Async XLA Ops:
  183.9 2.6 %copy-start.2 = (f32[128,128]{1,0:T(8,128)S(1)}, f32[128,128]{1,0:T(8,128)}, u32[]{:S(2)}) copy-start(f32[128,128]{1,0:T(8,128)} %get-tuple-element.9) | copy-start | bytes 196612
  183.9 3.2 %copy-start = (f32[1152,128]{1,0:T(8,128)S(1)}, f32[1152,128]{1,0:T(8,128)}, u32[]{:S(2)}) copy-start(f32[1152,128]{1,0:T(8,128)} %get-tuple-element.10) | copy-start | bytes 1769476
  183.9 4.0 %copy-start.1 = (f32[128,128]{1,0:T(8,128)S(1)}, f32[128,128]{1,0:T(8,128)}, u32[]{:S(2)}) copy-start(f32[128,128]{1,0:T(8,128)} %get-tuple-element.11) | copy-start | bytes 196612
